TPU v7x, 256 devices: a whole 4x4x8 slice. The times are simulated.
256 devices in a mesh: dp: 4 (over x), expert: 64 (over y, z, core).
Axes of the slice: x: 4, y: 4, z: 8, core: 2. Of those that a mesh axis runs over, the one named last changes fastest.
Arguments:
- tokens: bfloat16 [16384, 2048], P(('dp', 'expert')), may hold values from -6 to 6
- expert_ids: int32 [16384, 8], P(('dp', 'expert')), may hold values from 0 to 63, all different within a row; in each aligned block of 64 rows (0 to 63, 64 to 127, ...) at most 9 rows name the same one
- gates: float32 [16384, 8], P(('dp', 'expert')), may hold values from 0.1 to 0.5
- cotangent: bfloat16 [16384, 2048], P(('dp', 'expert')), may hold values from -6 to 6
- w_gate: bfloat16 [64, 2048, 768], P('expert'), may hold values from -0.125 to 0.125
- w_up: bfloat16 [64, 2048, 768], P('expert'), may hold values from -0.125 to 0.125
- w_down: bfloat16 [64, 768, 2048], P('expert'), may hold values from -0.21875 to 0.21875
Outputs:
- mixed: bfloat16 [16384, 2048], P(('dp', 'expert'))
- grad_tokens: bfloat16 [16384, 2048], P(('dp', 'expert'))
- grad_weights: bfloat16 [64, 768, 3, 2048], P('expert', 'dp')
Inputs may be any that keep to these rules, and one draw needn't show every extreme that they name: `expert_ids`: each token names 8 different experts. Among the tokens of one device (aligned blocks of 64 rows) no expert is named more than 9 times, and in every draw some expert is named exactly 9 times by the tokens of some device.
All inputs are finite; a program needn't handle non-finite values.
Results may differ from a plain program's by a relative error of at most 0.015.
Values may be sent and summed in bfloat16 or wider, within the bound.
A program may use at most 128 MiB of HBM per device.

v0:
```python
import jax
import jax.numpy as jnp
from jax import lax
from jax.sharding import PartitionSpec as P


def contract_rows(left, right):
    return lax.dot_general(
        left, right, (((0,), (0,)), ((), ())), preferred_element_type=jnp.float32
    )


def contract_cols(left, right):
    return lax.dot_general(
        left, right, (((1,), (1,)), ((), ())), preferred_element_type=jnp.float32
    )


def local(tokens, expert_ids, gates, cotangent, w_gate, w_up, w_down):
    tok_dev = tokens.shape[0]
    width = tokens.shape[1]
    choose = expert_ids.shape[1]
    n_experts = lax.axis_size("expert")
    n_replicas = lax.axis_size("dp")
    capacity = max(2, min(tok_dev, 9 * tok_dev * choose // (8 * n_experts)))
    pairs = tok_dev * choose
    padded = n_experts * capacity
    flat_ids = expert_ids.reshape(pairs)
    onehot = (flat_ids[:, None] == jnp.arange(n_experts, dtype=jnp.int32)[None, :]).astype(
        jnp.int32
    )
    slot = jnp.sum((jnp.cumsum(onehot, axis=0) - onehot) * onehot, axis=1)
    target = flat_ids * capacity + slot
    repeated = jnp.repeat(tokens, choose, axis=0)
    outgoing = jnp.zeros((padded, width), jnp.bfloat16).at[target].set(repeated)
    expert_in = lax.all_to_all(
        outgoing.reshape(n_experts, capacity, width),
        "expert",
        split_axis=0,
        concat_axis=0,
        tiled=True,
    ).reshape(padded, width)
    gate_w = w_gate[0]
    up_w = w_up[0]
    down_w = w_down[0]
    gate_pre = jnp.dot(expert_in, gate_w, preferred_element_type=jnp.float32)
    up_pre = jnp.dot(expert_in, up_w, preferred_element_type=jnp.float32)
    sigma = jax.nn.sigmoid(gate_pre)
    active = gate_pre * sigma
    hidden = (active * up_pre).astype(jnp.bfloat16)
    expert_out = jnp.dot(hidden, down_w, preferred_element_type=jnp.float32).astype(jnp.bfloat16)
    returned = lax.all_to_all(
        expert_out.reshape(n_experts, capacity, width),
        "expert",
        split_axis=0,
        concat_axis=0,
        tiled=True,
    ).reshape(padded, width)
    picked = returned[target].reshape(tok_dev, choose, width)
    mixed = jnp.sum(gates[:, :, None] * picked.astype(jnp.float32), axis=1).astype(jnp.bfloat16)
    routed = (
        (gates[:, :, None] * cotangent[:, None, :].astype(jnp.float32))
        .astype(jnp.bfloat16)
        .reshape(pairs, width)
    )
    routed_out = jnp.zeros((padded, width), jnp.bfloat16).at[target].set(routed)
    routed_in = lax.all_to_all(
        routed_out.reshape(n_experts, capacity, width),
        "expert",
        split_axis=0,
        concat_axis=0,
        tiled=True,
    ).reshape(padded, width)
    hidden_grad = contract_cols(routed_in, down_w)
    gate_grad = (hidden_grad * up_pre * sigma * (1.0 + gate_pre * (1.0 - sigma))).astype(
        jnp.bfloat16
    )
    up_grad = (hidden_grad * active).astype(jnp.bfloat16)
    slot_grad = (contract_cols(gate_grad, gate_w) + contract_cols(up_grad, up_w)).astype(
        jnp.bfloat16
    )
    back_rows = lax.all_to_all(
        slot_grad.reshape(n_experts, capacity, width),
        "expert",
        split_axis=0,
        concat_axis=0,
        tiled=True,
    ).reshape(padded, width)
    gathered_grads = back_rows[target].reshape(tok_dev, choose, width)
    grad_tokens = jnp.sum(gathered_grads.astype(jnp.float32), axis=1).astype(jnp.bfloat16)
    hidden_units = gate_w.shape[1]
    unit_share = hidden_units // n_replicas
    summed = (
        lax.psum_scatter(
            jnp.concatenate(
                [
                    contract_rows(gate_grad, expert_in),
                    contract_rows(up_grad, expert_in),
                    contract_rows(hidden, routed_in),
                ],
                axis=1,
            ).astype(jnp.bfloat16),
            "dp",
            scatter_dimension=0,
            tiled=True,
        )
        .astype(jnp.float32)
        .reshape(unit_share, 3, width)
    )
    grad_weights = summed.astype(jnp.bfloat16)[None]
    return (mixed, grad_tokens, grad_weights)


def solution(mesh):
    return jax.shard_map(
        local,
        mesh=mesh,
        in_specs=(
            P(("dp", "expert"), None),
            P(("dp", "expert"), None),
            P(("dp", "expert"), None),
            P(("dp", "expert"), None),
            P("expert", None, None),
            P("expert", None, None),
            P("expert", None, None),
        ),
        out_specs=(
            P(("dp", "expert"), None),
            P(("dp", "expert"), None),
            P("expert", "dp", None, None),
        ),
        check_vma=False,
    )
```

profile of v0, /device:TPU:1, one launch (start us, length us, event | category | flops | bytes accessed | tf_op | source)
XLA Modules:
  0.0 511.8 jit_solution(8965854931616575927)
XLA Ops:
  7.2 0.8 broadcast_multiply_fusion
  8.0 0.9 copy.14
  8.9 0.1 eq.25
  9.0 0.1 eq.29
  9.1 0.1 copy.13
  9.2 0.1 mul.69
  9.3 1.2 reduce-window.6
  10.5 0.2 slice_reduce_fusion
  10.8 1.8 convert_element_type.61
  12.5 0.8 copy.12
  13.3 0.1 mul.74
  13.4 0.1 fusion.31
  13.5 5.8 %scatter_custom_fusion.1 = bf16[576,2048]{1,0:T(8,128)(2,1)} fusion(s32[512]{0:T(512)S(1)} %bitcast.68, f32[64,2048]{1,0:T(8,128)} %convert_element_type.61, f32[512]{0:T(512)S(1)} %mul.74, bf16[]{:T(256)} %constant.6.clone.1), kind=kCustom, calls=%fused_computation.26 | custom fusion | flops 2097152 | bytes 2885634 | tf_op jit(solution)/shard_map/scatter | solution.py:66
  19.3 4.6 reshape.109
  23.9 13.3 %all-to-all-start.2 = ((bf16[64,9,2048]{2,1,0:T(8,128)(2,1)}), bf16[64,9,2048]{2,1,0:T(8,128)(2,1)}, u32[]{:S(2)}, u32[]{:S(2)}) async-start(bf16[64,9,2048]{2,1,0:T(8,128)(2,1)} %reshape.109), calls=%async_computation.2 | async-start | bytes 8388608 | tf_op jit(solution)/shard_map/all_to_all | solution.py:67
  37.3 5.6 %scatter_custom_fusion = bf16[576,2048]{1,0:T(8,128)(2,1)} fusion(s32[512]{0:T(512)S(1)} %bitcast.69, bf16[]{:T(256)} %constant.6.clone.1, bf16[64,2048]{1,0:T(8,128)(2,1)} %param.7), kind=kCustom, calls=%fused_computation.28 | custom fusion | bytes 2621442 | tf_op jit(solution)/shard_map/scatter | solution.py:35
  42.9 4.6 reshape.105
  47.5 85.7 %all-to-all-done.2 = bf16[64,9,2048]{2,1,0:T(8,128)(2,1)} async-done(((bf16[64,9,2048]{2,1,0:T(8,128)(2,1)}), bf16[64,9,2048]{2,1,0:T(8,128)(2,1)}, u32[]{:S(2)}, u32[]{:S(2)}) %all-to-all-start.2) | async-done | bytes 2359328 | tf_op jit(solution)/shard_map/all_to_all | solution.py:67
  133.2 5.9 %all-to-all-start = ((bf16[64,9,2048]{2,1,0:T(8,128)(2,1)}), bf16[64,9,2048]{2,1,0:T(8,128)(2,1)}, u32[]{:S(2)}, u32[]{:S(2)}) async-start(bf16[64,9,2048]{2,1,0:T(8,128)(2,1)} %reshape.105), calls=%async_computation | async-start | bytes 8388608 | tf_op jit(solution)/shard_map/all_to_all | solution.py:36
  139.1 0.2 reduce-scatter.2.cloned.1.call-start
  139.3 4.7 reshape.110
  144.0 5.9 %fusion.2 = f32[576,768]{1,0:T(8,128)} fusion(bf16[576,2048]{1,0:T(8,128)(2,1)} %reshape.110, bf16[1,768,2048]{2,1,0:T(8,128)(2,1)} %param.13), kind=kOutput, calls=%fused_computation.13 | convolution fusion | flops 1811939328 | bytes 7274496 | tf_op jit(solution)/shard_map/dot_general | solution.py:14
  149.9 85.1 %all-to-all-done = bf16[64,9,2048]{2,1,0:T(8,128)(2,1)} async-done(((bf16[64,9,2048]{2,1,0:T(8,128)(2,1)}), bf16[64,9,2048]{2,1,0:T(8,128)(2,1)}, u32[]{:S(2)}, u32[]{:S(2)}) %all-to-all-start) | async-done | bytes 2359328 | tf_op jit(solution)/shard_map/all_to_all | solution.py:36
  235.0 4.7 reshape.106
  239.7 4.7 fusion.8
  244.5 2.7 multiply_convert_fusion.1
  247.2 2.9 convolution_convert_fusion
  250.1 2.9 convolution_convert_fusion.1
  253.0 2.9 convolution_convert_fusion.2
  255.9 4.1 pad_maximum_fusion
  260.0 0.0 reduce-scatter.2.cloned.1.call-update
  260.0 5.6 %fusion.14 = bf16[576,2048]{1,0:T(8,128)(2,1)} fusion(bf16[576,768]{1,0:T(8,128)(2,1)} %copy-done.7, bf16[1,768,2048]{2,1,0:T(8,128)(2,1)} %param.13), kind=kOutput, calls=%fused_computation.25 | convolution fusion | flops 1813118976 | bytes 6389760 | tf_op jit(solution)/shard_map/dot_general | solution.py:51
  265.6 4.9 reshape.107
  270.4 5.6 %all-to-all-start.1 = ((bf16[64,9,2048]{2,1,0:T(8,128)(2,1)}), bf16[64,9,2048]{2,1,0:T(8,128)(2,1)}, u32[]{:S(2)}, u32[]{:S(2)}) async-start(bf16[64,9,2048]{2,1,0:T(8,128)(2,1)} %reshape.107), calls=%async_computation.1 | async-start | bytes 8388608 | tf_op jit(solution)/shard_map/all_to_all | solution.py:52
  276.1 4.3 fusion.6
  280.4 3.5 add_convert_fusion
  283.8 4.7 reshape.111
  288.5 83.5 %all-to-all-done.1 = bf16[64,9,2048]{2,1,0:T(8,128)(2,1)} async-done(((bf16[64,9,2048]{2,1,0:T(8,128)(2,1)}), bf16[64,9,2048]{2,1,0:T(8,128)(2,1)}, u32[]{:S(2)}, u32[]{:S(2)}) %all-to-all-start.1) | async-done | bytes 2359328 | tf_op jit(solution)/shard_map/all_to_all | solution.py:52
  372.0 5.9 %all-to-all-start.3 = ((bf16[64,9,2048]{2,1,0:T(8,128)(2,1)}), bf16[64,9,2048]{2,1,0:T(8,128)(2,1)}, u32[]{:S(2)}, u32[]{:S(2)}) async-start(bf16[64,9,2048]{2,1,0:T(8,128)(2,1)} %reshape.111), calls=%async_computation.3 | async-start | bytes 8388608 | tf_op jit(solution)/shard_map/all_to_all | solution.py:82
  377.9 4.7 reshape.108
  382.6 7.2 %gather_fusion = bf16[512,2048]{1,0:T(8,128)(2,1)} fusion(bf16[576,2048]{1,0:T(8,128)(2,1)} %reshape.108, s32[1024]{0:T(1024)S(1)} %pad_clamp_fusion), kind=kCustom, calls=%fused_computation | custom fusion | bytes 4196352 | tf_op jit(solution)/shard_map/gather | solution.py:59
  389.8 84.0 %all-to-all-done.3 = bf16[64,9,2048]{2,1,0:T(8,128)(2,1)} async-done(((bf16[64,9,2048]{2,1,0:T(8,128)(2,1)}), bf16[64,9,2048]{2,1,0:T(8,128)(2,1)}, u32[]{:S(2)}, u32[]{:S(2)}) %all-to-all-start.3) | async-done | bytes 2359328 | tf_op jit(solution)/shard_map/all_to_all | solution.py:82
  473.8 4.7 reshape.112
  478.5 7.3 %gather_fusion.1 = bf16[512,2048]{1,0:T(8,128)(2,1)} fusion(bf16[576,2048]{1,0:T(8,128)(2,1)} %reshape.112, s32[1024]{0:T(1024)S(1)} %pad_clamp_fusion), kind=kCustom, calls=%fused_computation.1 | custom fusion | bytes 4196352 | tf_op jit(solution)/shard_map/gather | solution.py:89
  485.8 3.9 bitcast_reduce_fusion
  489.6 2.6 fusion
  492.2 7.4 %convert_element_type.66 = bf16[1,192,3,2048]{3,2,1,0:T(4,128)(2,1)} reshape(bf16[192,6144]{1,0:T(8,128)(2,1)} %reduce-scatter.2.cloned.1.call-done) | data formatting | bytes 4718592 | tf_op jit(solution)/shard_map/convert_element_type | solution.py:110
  499.6 5.0 copy.18
  (24 shorter events, 0.1 us)
Async XLA Ops:
  7.2 237.3 %copy-start = (bf16[1,2048,768]{2,1,0:T(8,128)(2,1)S(1)}, bf16[1,2048,768]{2,1,0:T(8,128)(2,1)}, u32[]{:S(2)}) copy-start(bf16[1,2048,768]{2,1,0:T(8,128)(2,1)} %param.11) | copy-start | bytes 9437188
  23.9 109.2 %all-to-all-start.2 = ((bf16[64,9,2048]{2,1,0:T(8,128)(2,1)}), bf16[64,9,2048]{2,1,0:T(8,128)(2,1)}, u32[]{:S(2)}, u32[]{:S(2)}) async-start(bf16[64,9,2048]{2,1,0:T(8,128)(2,1)} %reshape.109), calls=%async_computation.2 | async-start | bytes 8388608 | tf_op jit(solution)/shard_map/all_to_all | solution.py:67
  133.2 101.8 %all-to-all-start = ((bf16[64,9,2048]{2,1,0:T(8,128)(2,1)}), bf16[64,9,2048]{2,1,0:T(8,128)(2,1)}, u32[]{:S(2)}, u32[]{:S(2)}) async-start(bf16[64,9,2048]{2,1,0:T(8,128)(2,1)} %reshape.105), calls=%async_computation | async-start | bytes 8388608 | tf_op jit(solution)/shard_map/all_to_all | solution.py:36
  139.1 353.0 %reduce-scatter.2.cloned.1.call-start = ((), (), s32[]{:S(2)}) async-start(), calls=%async_computation.5 | async-start | bytes 11796480 | tf_op jit(solution)/shard_map/reduce_scatter | solution.py:94
  239.7 4.8 copy-start.3
  239.7 4.8 copy-start.8
  244.5 2.7 copy-start.2
  247.1 2.9 copy-start.7
  247.2 2.9 copy-start.4
  247.2 5.8 %copy-start.5 = (bf16[576,768]{1,0:T(8,128)(2,1)}, bf16[576,768]{1,0:T(8,128)(2,1)S(1)}, u32[]{:S(2)}) copy-start(bf16[576,768]{1,0:T(8,128)(2,1)S(1)} %get-tuple-element.9) | copy-start | bytes 2654212
  270.4 101.5 %all-to-all-start.1 = ((bf16[64,9,2048]{2,1,0:T(8,128)(2,1)}), bf16[64,9,2048]{2,1,0:T(8,128)(2,1)}, u32[]{:S(2)}, u32[]{:S(2)}) async-start(bf16[64,9,2048]{2,1,0:T(8,128)(2,1)} %reshape.107), calls=%async_computation.1 | async-start | bytes 8388608 | tf_op jit(solution)/shard_map/all_to_all | solution.py:52
  276.1 4.3 copy-start.6
  372.0 101.8 %all-to-all-start.3 = ((bf16[64,9,2048]{2,1,0:T(8,128)(2,1)}), bf16[64,9,2048]{2,1,0:T(8,128)(2,1)}, u32[]{:S(2)}, u32[]{:S(2)}) async-start(bf16[64,9,2048]{2,1,0:T(8,128)(2,1)} %reshape.111), calls=%async_computation.3 | async-start | bytes 8388608 | tf_op jit(solution)/shard_map/all_to_all | solution.py:82
  485.8 3.9 copy-start.1
Sparse Core Ops, SparseCore 0:
  260.1 87.9 reduce-scatter.1
where the time goes:
time: 521 us; the launch traced here: 512 us
  waiting for transfers between devices  338 us (65%)
  local copies, waits for them, and re-layouts  72.3 us (14%)
  matrix products  35.2 us (7%)
  starting transfers between devices  31.1 us (6%)
  other arithmetic  20.3 us (4%)
  between operations  14.6 us (3%)
    all_to_all x1, waiting for transfers between devices, local(): lax.all_to_all(routed_out.reshape(n_experts, capacity, width), 'expert',...  85.7 us
    all_to_all x1, waiting for transfers between devices, local(): lax.all_to_all(outgoing.reshape(n_experts, capacity, width), 'expert', sp...  85.1 us
    all_to_all x1, waiting for transfers between devices, local(): lax.all_to_all(slot_grad.reshape(n_experts, capacity, width), 'expert', s...  84 us
    all_to_all x1, waiting for transfers between devices, local(): lax.all_to_all(expert_out.reshape(n_experts, capacity, width), 'expert',...  83.5 us
    dot_general x3, matrix products, contract_cols(): lax.dot_general(left, right, (((1,), (1,)), ((), ())), preferred_element_...  13.6 us
    all_to_all x1, starting transfers between devices, local(): lax.all_to_all(routed_out.reshape(n_experts, capacity, width), 'expert',...  13.3 us
  transfers between devices with their start and end apart: 5, of which 4 were waited for; matrix products, arithmetic and copies ran while one was open for 14% of the time, Pallas kernels for 0%

commit v1 on v0

v1 whole, which is shorter than its diff:
```python
import jax
import jax.numpy as jnp
from jax import lax
from jax.experimental import pallas as pl
from jax.experimental.pallas import tpu as pltpu
from jax.sharding import PartitionSpec as P

MESH = pl.DeviceIdType.MESH
BF = jnp.bfloat16
F32 = jnp.float32

NX, NY, NZ = 4, 4, 8
D, FF, TOK, TOP, CAP = 2048, 768, 64, 8, 9
HALF = D // 2
BLK = 16 * CAP
ROWS = NY * BLK
SHARE = FF // NX
QC = 512
NQ = HALF // QC
ORDER = (2, 6, 4, 3, 7, 5, 1, 0)


def dot(a, b, ca, cb):
    return lax.dot_general(a, b, (((ca,), (cb,)), ((), ())), preferred_element_type=F32)


def kernel(
    tok, cot, ids, gates, wg_h, wu_h, wd_h,
    mixed_o, gtok_o, gw_o,
    T, S, meta_s, meta_r, pos, gat, yb, xin, wg, wu, wd, act, ret, zr, G, xr1, xr2, tw,
    w_sem, tws, twr, tls, ms, mr, zs, zrv, ys, yr, rs, rr, zbs, zbr, xs, xrv, os_, orv, ol,
):
    x = lax.axis_index("dp")
    e = lax.axis_index("expert")
    y, z, c = e // 16, lax.rem(e // 2, NZ), lax.rem(e, 2)

    def at(dx, dy, dz, dc):
        return (
            lax.rem(x + dx + NX, NX),
            (lax.rem(y + dy + NY, NY) * NZ + lax.rem(z + dz + NZ, NZ)) * 2 + lax.rem(c + dc, 2),
        )

    def remote(src, dst, ssem, rsem, where):
        return pltpu.make_async_remote_copy(
            src_ref=src, dst_ref=dst, send_sem=ssem, recv_sem=rsem,
            device_id=where, device_id_type=MESH,
        )

    w_in = [
        pltpu.make_async_copy(src, dst, w_sem.at[i])
        for i, (src, dst) in enumerate(((wg_h, wg), (wu_h, wu), (wd_h, wd)))
    ]
    for cp in w_in:
        cp.start()

    greet = [(0, 0, dz, dc) for dz in range(NZ) for dc in range(2) if dz or dc]
    greet += [(0, dy, 0, dc) for dy in range(1, NY) for dc in range(2)]
    greet += [(1, 0, 0, 0), (-1, 0, 0, 0)]
    bar = pltpu.get_barrier_semaphore()
    for g in greet:
        pl.semaphore_signal(bar, inc=1, device_id=at(*g), device_id_type=MESH)
    pl.semaphore_wait(bar, len(greet))

    def zrow(dz, lo=0, n=128):
        return pl.ds(pl.multiple_of(lax.rem(z + dz + NZ, NZ) * 128 + lo, 16), n)

    mine = pl.ds(pl.multiple_of(c * HALF, HALF), HALF)
    other = pl.ds(pl.multiple_of((1 - c) * HALF, HALF), HALF)

    swaps, keeps = [], []
    for a, src in enumerate((tok, cot)):
        rows = pl.ds(pl.multiple_of(z * 128 + c * TOK, TOK), TOK)
        cp = remote(src.at[:, other], T.at[a, rows, :], tws.at[a], twr.at[a], at(0, 0, 0, 1))
        cp.start()
        swaps.append(cp)
        cp = pltpu.make_async_copy(src.at[:, mine], T.at[a, rows, :], tls.at[a])
        cp.start()
        keeps.append(cp)

    idv = ids[...]
    place = ((idv >> 1) & 7) * 8 + (idv >> 4) * 2 + (idv & 1)
    lane = lax.broadcasted_iota(jnp.int32, (TOK, 64), 1)
    named = jnp.zeros((TOK, 64), F32)
    gated = jnp.zeros((TOK, 64), F32)
    for k in range(TOP):
        hit = place[:, k : k + 1] == lane
        named = named + jnp.where(hit, 1.0, 0.0)
        gated = gated + jnp.where(hit, gates[:, k : k + 1], 0.0)
    t0 = lax.broadcasted_iota(jnp.int32, (TOK, 128), 0)
    l0 = lax.broadcasted_iota(jnp.int32, (TOK, 128), 1) - TOK * c
    same = jnp.where(t0 == l0, 1.0, 0.0).astype(BF)
    upto = jnp.where(t0 <= l0, jnp.where(l0 < TOK, 1.0, 0.0), 0.0).astype(BF)
    named = named.astype(BF)
    rank = dot(named, upto, 0, 0) * dot(named, same, 0, 0)
    gate_t = dot(gated.astype(BF), same, 0, 0)
    for k in range(NZ):
        meta_s[k, 0:8, :] = rank[k * 8 : k * 8 + 8]
        meta_s[k, 8:16, :] = gate_t[k * 8 : k * 8 + 8]
    metas = []
    for dz in (1, 7, 2, 6, 3, 5, 4, 0):
        for dc in (0, 1):
            src = meta_s.at[lax.rem(z + dz, NZ)]
            dst = meta_r.at[z * 2 + c]
            if dz == 0 and dc == 0:
                cp = pltpu.make_async_copy(src, dst, mr.at[0, 0])
            else:
                cp = remote(src, dst, ms.at[dz, dc], mr.at[dz, dc], at(0, 0, dz, dc))
            cp.start()
            metas.append((cp, dz or dc))

    def zcopy(p, q, s, way):
        a = p // NQ
        cols = pl.ds((p % NQ) * QC + q * (QC // 2), QC // 2)
        rows = zrow(-s * way) if s < 3 else zrow(-3 * way, 0 if way == 1 else 64, 64)
        i = 0 if way == 1 else 1
        return remote(
            T.at[a, rows, cols], T.at[a, rows, cols],
            zs.at[p, q, s, i], zrv.at[p, q, s, i], at(0, 0, way, 0),
        )

    zc = {
        (p, q, s, w): zcopy(p, q, s, w)
        for p in range(2 * NQ) for q in range(2) for s in range(4) for w in (1, -1)
    }

    def zstart(p, s):
        for q in range(2):
            for w in (1, -1):
                if s:
                    zc[p, q, s - 1, w].wait_recv()
                zc[p, q, s, w].start()

    def target(r):
        return at(0, r // 2, 0, r % 2)

    my_rows = pl.ds(pl.multiple_of(y * BLK, 16), BLK)

    def ycopy(p, r):
        a, q = p // NQ, p % NQ
        src = yb.at[a, pl.ds(r * BLK, BLK), pl.ds(q * QC, QC)]
        dst = xin.at[a, my_rows, pl.ds(pl.multiple_of(c * HALF + q * QC, QC), QC)]
        if r == 0:
            return pltpu.make_async_copy(src, dst, yr.at[p, 0])
        return remote(src, dst, ys.at[p, r], yr.at[p, r], target(r))

    yc = {(p, r): ycopy(p, r) for p in range(2 * NQ) for r in range(8)}

    def select(p, r):
        a, q = p // NQ, p % NQ
        rows = dot(S[a, r * BLK : (r + 1) * BLK, :], T[a, :, q * QC : (q + 1) * QC], 1, 0)
        yb[a, r * BLK : (r + 1) * BLK, q * QC : (q + 1) * QC] = rows.astype(BF)
        yc[p, r].start()

    for a in range(2):
        swaps[a].wait_recv()
        keeps[a].wait()
    zstart(0, 0)

    for cp, far in metas:
        if far:
            cp.wait_recv()
        else:
            cp.wait()
    lane8 = lax.broadcasted_iota(jnp.int32, (8, 128), 1)
    for k in range(NZ):
        enc = meta_r[2 * k, 0:8, :] + meta_r[2 * k + 1, 0:8, :]
        base = jnp.where(lane8 < TOK, 2.0 * k * CAP - 1.0, (2.0 * k + 1.0) * CAP - 1.0)
        pos[:, k * 128 : (k + 1) * 128] = jnp.where(enc > 0.5, enc + base, -1.0)
        gat[:, k * 128 : (k + 1) * 128] = meta_r[2 * k, 8:16, :] + meta_r[2 * k + 1, 8:16, :]
    zstart(0, 1)
    row16 = lax.broadcasted_iota(jnp.int32, (16, 16 * TOK), 0).astype(F32)

    def build(r, carry):
        j = lax.rem(y + r // 2, NY) * 2 + lax.rem(c + r, 2)
        prow = pos[pl.ds(j, 1), :]
        grow = gat[pl.ds(j, 1), :]
        for i in range(BLK // 16):
            hit = row16 + float(16 * i) == prow
            at_rows = pl.ds(pl.multiple_of(r * BLK + 16 * i, 16), 16)
            S[0, at_rows, :] = jnp.where(hit, 1.0, 0.0).astype(BF)
            S[1, at_rows, :] = jnp.where(hit, grow, 0.0).astype(BF)
        return carry

    lax.fori_loop(0, 8, build, 0)

    NP = 2 * NQ
    for p in range(NP + 1):
        for s in range(4):
            if p < NP and s >= (2 if p == 0 else 1):
                zstart(p, s)
            if s == 3 and p + 1 < NP:
                zstart(p + 1, 0)
            if p:
                for r in ORDER[2 * s : 2 * s + 2]:
                    select(p - 1, r)
        if p < NP:
            for q in range(2):
                for w in (1, -1):
                    zc[p, q, 3, w].wait_recv()

    def arrived(a):
        for p in range(a * NQ, a * NQ + NQ):
            for r in range(8):
                if r:
                    yc[p, r].wait_recv()
                    yc[p, r].wait_send()
                else:
                    yc[p, r].wait()

    arrived(0)
    for cp in w_in:
        cp.wait()
    HR = ROWS // 2

    def forward(i, carry):
        rows = pl.ds(pl.multiple_of(lax.rem(i, 2) * HR, 16), HR)
        cols = pl.ds(pl.multiple_of((i // 2) * 256, 256), 256)
        v = xin[0, rows, :]
        g = dot(v, wg[:, cols], 1, 0)
        u = dot(v, wu[:, cols], 1, 0)
        sg = jax.nn.sigmoid(g)
        silu = g * sg
        act[0, rows, cols] = (silu * u).astype(BF)
        act[1, rows, cols] = (u * sg * (1.0 + g * (1.0 - sg))).astype(BF)
        act[2, rows, cols] = silu.astype(BF)
        return carry

    lax.fori_loop(0, 2 * FF // 256, forward, 0)

    def give_back(a, q, h, rows):
        for k in range(NY):
            r = lax.rem(k - y + NY, NY) * 2 + lax.rem(h - c + 2, 2)
            yb[a, pl.ds(pl.multiple_of(r * BLK, 16), BLK), q * QC : (q + 1) * QC] = (
                rows[k * BLK : (k + 1) * BLK].astype(BF)
            )

    def rcopy(a, q, r):
        cols = pl.ds(q * QC, QC)
        there = (NY - r // 2) % NY * 2 + r % 2
        src = yb.at[a, pl.ds(r * BLK, BLK), cols]
        dst = ret.at[a, pl.ds(there * BLK, BLK), cols]
        if r == 0:
            return pltpu.make_async_copy(src, dst, rr.at[a, q, 0])
        return remote(src, dst, rs.at[a, q, r], rr.at[a, q, r], target(r))

    rc = {(a, q, r): rcopy(a, q, r) for a in range(2) for q in range(NQ) for r in range(8)}

    for q in range(NQ):
        for h in range(2):
            n = h * HALF + q * QC
            give_back(0, q, h, dot(act[0], wd[:, n : n + QC], 1, 0))

    def xshare(dx):
        return lax.rem(x + dx + NX, NX)

    SH2 = SHARE // 2

    def xcopy1(m, way):
        i = 0 if way == 1 else 1
        return remote(
            G.at[xshare(2), m, pl.ds(i * SH2, SH2), :], xr1.at[i, m],
            xs.at[0, m, i], xrv.at[0, m, i], at(way, 0, 0, 0),
        )

    def xcopy2(m, way):
        i = 0 if way == 1 else 1
        return remote(
            G.at[xshare(way), m], xr2.at[i, m],
            xs.at[1, m, i], xrv.at[1, m, i], at(way, 0, 0, 0),
        )

    xc1 = {(m, w): xcopy1(m, w) for m in range(3) for w in (1, -1)}
    xc2 = {(m, w): xcopy2(m, w) for m in range(3) for w in (1, -1)}

    def weights(m, b, k):
        def part(i, carry):
            cols = pl.ds(pl.multiple_of(i * QC, QC), QC)
            for hf in range(2):
                v = dot(act[k, :, hf * 384 : (hf + 1) * 384], xin[b, :, cols], 0, 0).astype(BF)
                G[2 * hf, m, :, cols] = v[:SHARE]
                G[2 * hf + 1, m, :, cols] = v[SHARE:]
            return carry

        lax.fori_loop(0, D // QC, part, 0)
        for w in (1, -1):
            xc1[m, w].start()

    arrived(1)
    for q in range(NQ):
        for r in ORDER:
            rc[0, q, r].start()
    weights(2, 1, 0)

    def backward(i, carry):
        cols = pl.ds(pl.multiple_of(i * 256, 256), 256)
        g = dot(xin[1], wd[cols, :], 1, 1)
        act[1, :, cols] = (g * act[1, :, cols].astype(F32)).astype(BF)
        act[2, :, cols] = (g * act[2, :, cols].astype(F32)).astype(BF)
        return carry

    lax.fori_loop(0, FF // 256, backward, 0)
    weights(0, 0, 1)
    weights(1, 0, 2)
    for q in range(NQ):
        for h in range(2):
            n = h * HALF + q * QC
            give_back(
                1, q, h,
                dot(act[1], wg[n : n + QC, :], 1, 1) + dot(act[2], wu[n : n + QC, :], 1, 1),
            )
        for r in ORDER:
            rc[1, q, r].start()

    def xadd(m):
        for i, w in enumerate((1, -1)):
            xc1[m, w].wait_recv()
            rows = pl.ds(i * SH2, SH2)
            d = xshare(w)
            G[d, m, rows, :] = (G[d, m, rows, :].astype(F32) + xr1[i, m].astype(F32)).astype(BF)
            xc2[m, w].start()

    for a in range(2):
        swaps[a].wait_send()
    for key in zc:
        zc[key].wait_send()

    def bcopy(a, q, s, way):
        i = 0 if way == 1 else 1
        cols = pl.ds(q * QC, QC)
        rows = zrow((4 - s) * way) if s else zrow(4, 64 * i, 64)
        dst = zr.at[a, i, s, :, cols] if s else zr.at[a, i, 0, pl.ds(0, 64), cols]
        return remote(
            T.at[a, rows, cols], dst, zbs.at[a, q, s, i], zbr.at[a, q, s, i], at(0, 0, way, 0)
        )

    def combine(a, q):
        for r in range(8):
            if r:
                rc[a, q, r].wait_recv()
            else:
                rc[a, q, r].wait()
        cols = slice(q * QC, (q + 1) * QC)
        for k in range(NZ):
            v = dot(S[1 - a, :, k * 128 : (k + 1) * 128], ret[a, :, cols], 0, 0)
            T[a, k * 128 : (k + 1) * 128, cols] = v.astype(BF)
        done = []
        for s in range(4):
            for i, w in enumerate((1, -1)):
                if s:
                    done[2 * (s - 1) + i].wait_recv()
                    n = 64 if s == 1 else 128
                    rows = zrow((4 - s) * w, 64 * i if s == 1 else 0, n)
                    T[a, rows, cols] = (
                        T[a, rows, cols].astype(F32) + zr[a, i, s - 1, 0:n, cols].astype(F32)
                    ).astype(BF)
                cp = bcopy(a, q, s, w)
                cp.start()
                done.append(cp)
        return done

    def finish(a, q, done):
        cols = slice(q * QC, (q + 1) * QC)
        for cp in done[6:]:
            cp.wait_recv()
        rows = zrow(0)
        T[a, rows, cols] = (
            T[a, rows, cols].astype(F32)
            + zr[a, 0, 3, :, cols].astype(F32)
            + zr[a, 1, 3, :, cols].astype(F32)
        ).astype(BF)

    outs = (mixed_o, gtok_o)
    tail = []

    def hand_over(a):
        theirs = pl.ds(pl.multiple_of(z * 128 + (1 - c) * TOK, TOK), TOK)
        ours = pl.ds(pl.multiple_of(z * 128 + c * TOK, TOK), TOK)
        cp = remote(T.at[a, theirs, :], tw.at[a], os_.at[a], orv.at[a], at(0, 0, 0, 1))
        cp.start()
        keep = pltpu.make_async_copy(T.at[a, ours, :], outs[a].at[:, mine], ol.at[a])
        keep.start()
        return cp, keep

    def take_over(a, pair):
        cp, keep = pair
        cp.wait_recv()
        last = pltpu.make_async_copy(tw.at[a], outs[a].at[:, other], ol.at[2 + a])
        last.start()
        tail.extend((keep, last))

    sent = []
    xadd(2)
    d00 = combine(0, 0)
    xadd(0)
    d01 = combine(0, 1)
    finish(0, 0, d00)
    xadd(1)
    finish(0, 1, d01)
    pair0 = hand_over(0)
    d10 = combine(1, 0)
    take_over(0, pair0)
    d11 = combine(1, 1)
    finish(1, 0, d10)
    finish(1, 1, d11)
    pair1 = hand_over(1)
    take_over(1, pair1)
    for m in (2, 0, 1):
        for w in (1, -1):
            xc2[m, w].wait_recv()
        own = xshare(0)
        G[own, m] = (
            G[own, m].astype(F32) + xr2[0, m].astype(F32) + xr2[1, m].astype(F32)
        ).astype(BF)
        cp = pltpu.make_async_copy(G.at[own, m], gw_o.at[m], ol.at[4 + m])
        cp.start()
        tail.append(cp)

    for cp, far in metas:
        if far:
            cp.wait_send()
    for a in range(2):
        for q in range(NQ):
            for r in range(1, 8):
                rc[a, q, r].wait_send()
    for d in (d00, d01, d10, d11):
        for cp in d:
            cp.wait_send()
    for pair in (pair0, pair1):
        pair[0].wait_send()
    for m in range(3):
        for w in (1, -1):
            xc1[m, w].wait_send()
            xc2[m, w].wait_send()
    for cp in tail:
        cp.wait()


def local(tokens, expert_ids, gates, cotangent, w_gate, w_up, w_down):
    vmem = pl.BlockSpec(memory_space=pltpu.VMEM)
    hbm = pl.BlockSpec(memory_space=pl.ANY)
    dma = pltpu.SemaphoreType.DMA
    mixed, grad_tokens, grads = pl.pallas_call(
        kernel,
        out_shape=(
            jax.ShapeDtypeStruct((TOK, D), BF),
            jax.ShapeDtypeStruct((TOK, D), BF),
            jax.ShapeDtypeStruct((3, SHARE, D), BF),
        ),
        in_specs=[vmem] * 4 + [hbm] * 3,
        out_specs=(hbm, hbm, hbm),
        scratch_shapes=[
            pltpu.VMEM((2, 16 * TOK, HALF), BF),
            pltpu.VMEM((2, 8 * BLK, 16 * TOK), BF),
            pltpu.VMEM((NZ, 16, 128), F32),
            pltpu.VMEM((2 * NZ, 16, 128), F32),
            pltpu.VMEM((8, 16 * TOK), F32),
            pltpu.VMEM((8, 16 * TOK), F32),
            pltpu.VMEM((2, 8 * BLK, HALF), BF),
            pltpu.VMEM((2, ROWS, D), BF),
            pltpu.VMEM((D, FF), BF),
            pltpu.VMEM((D, FF), BF),
            pltpu.VMEM((FF, D), BF),
            pltpu.VMEM((3, ROWS, FF), BF),
            pltpu.VMEM((2, 8 * BLK, HALF), BF),
            pltpu.VMEM((2, 2, 4, 128, HALF), BF),
            pltpu.VMEM((NX, 3, SHARE, D), BF),
            pltpu.VMEM((2, 3, SHARE // 2, D), BF),
            pltpu.VMEM((2, 3, SHARE, D), BF),
            pltpu.VMEM((2, TOK, HALF), BF),
            dma((3,)), dma((2,)), dma((2,)), dma((2,)),
            dma((NZ, 2)), dma((NZ, 2)),
            dma((2 * NQ, 2, 4, 2)), dma((2 * NQ, 2, 4, 2)),
            dma((2 * NQ, 8)), dma((2 * NQ, 8)),
            dma((2, NQ, 8)), dma((2, NQ, 8)),
            dma((2, NQ, 4, 2)), dma((2, NQ, 4, 2)),
            dma((2, 3, 2)), dma((2, 3, 2)),
            dma((2,)), dma((2,)), dma((7,)),
        ],
        compiler_params=pltpu.CompilerParams(
            collective_id=0, has_side_effects=True, vmem_limit_bytes=60 * 2**20
        ),
        cost_estimate=pl.CostEstimate(
            flops=30_000_000_000, bytes_accessed=20_000_000, transcendentals=450_000
        ),
        name="moe",
    )(tokens, cotangent, expert_ids, gates, w_gate[0], w_up[0], w_down[0])
    return mixed, grad_tokens, grads.transpose(1, 0, 2)[None]


def solution(mesh):
    return jax.shard_map(
        local,
        mesh=mesh,
        in_specs=(
            P(("dp", "expert"), None),
            P(("dp", "expert"), None),
            P(("dp", "expert"), None),
            P(("dp", "expert"), None),
            P("expert", None, None),
            P("expert", None, None),
            P("expert", None, None),
        ),
        out_specs=(
            P(("dp", "expert"), None),
            P(("dp", "expert"), None),
            P("expert", "dp", None, None),
        ),
        check_vma=False,
    )
```

time: 521 us -> 186 us (0.36); the launches traced: 512 us -> 186 us
  waiting for transfers between devices: 338 us -> 0 us
  Pallas kernels: 0 us -> 176 us
  local copies, waits for them, and re-layouts: 72.3 us -> 9.46 us
  matrix products: 35.2 us -> 0 us
  starting transfers between devices: 31.1 us -> 0 us
  other arithmetic: 20.3 us -> 0 us
  between operations: 14.6 us -> 0.64 us
    all_to_all x4 -> x0, waiting for transfers between devices: 338 us -> none  [the longest x1 85.7 us: local(): lax.all_to_all(routed_out.reshape(n_experts, capacity, width), 'expert',...]
    pallas_call x0 -> x1, Pallas kernels: none -> 176 us  [local(): pl.pallas_call(kernel, out_shape=(jax.ShapeDtypeStruct((TOK, D), BF), jax...]
    reshape x8 -> x0, local copies, waits for them, and re-layouts: 37.4 us -> none  [the longest x1 4.89 us: local(): expert_out.reshape(n_experts, capacity, width)]
    dot_general x9 -> x0, matrix products: 35.2 us -> none  [the longest x3 13.6 us: contract_cols(): lax.dot_general(left, right, (((1,), (1,)), ((), ())), preferred_element_...]
    all_to_all x4 -> x0, starting transfers between devices: 30.9 us -> none  [the longest x1 13.3 us: local(): lax.all_to_all(routed_out.reshape(n_experts, capacity, width), 'expert',...]
    gather x2 -> x0, local copies, waits for them, and re-layouts: 14.5 us -> none  [the longest x1 7.27 us: local(): gathered_grads = back_rows[target].reshape(tok_dev, choose, width)]
    convert_element_type x1 -> x0, local copies, waits for them, and re-layouts: 7.39 us -> none  [local(): grad_weights = summed.astype(jnp.bfloat16)[None]]
    reduce_sum x3 -> x0, other arithmetic: 6.53 us -> none  [the longest x1 3.86 us: local(): jnp.sum(gathered_grads.astype(jnp.float32), axis=1).astype(jnp.bfloat16)]
  transfers between devices with their start and end apart: 5 -> 0, of which waited for: 4 -> 0; matrix products, arithmetic and copies ran while one was open for 14% -> 0% of each run, Pallas kernels for 0% -> 0%
where the time goes in v1:
time: 186 us
  Pallas kernels  176 us (95%)
  local copies, waits for them, and re-layouts  9.46 us (5%)
    pallas_call x1, Pallas kernels, local(): pl.pallas_call(kernel, out_shape=(jax.ShapeDtypeStruct((TOK, D), BF), jax...  176 us
    unnamed x5, local copies, waits for them, and re-layouts  9.46 us

profile of v1, /device:TPU:1, one launch (start us, length us, event | category | flops | bytes accessed | tf_op | source)
XLA Modules:
  0.0 186.2 jit_solution(5138799332596541363)
XLA Ops:
  0.6 1.4 copy.10.ids
  2.0 1.4 copy.11.gates
  3.4 176.1 %moe.1 = (bf16[64,2048]{1,0:T(8,128)(2,1)}, bf16[64,2048]{1,0:T(8,128)(2,1)}, bf16[3,192,2048]{2,1,0:T(8,128)(2,1)}) custom-call(bf16[64,2048]{1,0:T(8,128)(2,1)} %tok.1, bf16[64,2048]{1,0:T(8,128)(2,1)} %cot.1, s32[64,8]{1,0:T(8,128)} %copy.10.ids, f32[64,8]{1,0:T(8,128)} %copy.11.gates, bf16[2048,768]{1,0:T(8,128)(2,1)} %bitcast.7, ...), custom_call_target="tpu_custom_call" | custom-call | flops 30000001024 | bytes 20000000 | tf_op jit(solution)/shard_map/moe/pallas_call | solution.py:442
  179.5 1.7 copy.15
  181.2 1.7 copy.16
  182.8 3.4 %copy.17 = bf16[1,192,3,2048]{3,1,2,0:T(8,128)(2,1)} copy(bf16[1,192,3,2048]{3,1,2,0:T(8,128)(2,1)} %bitcast.6) | data formatting | bytes 4718592

commit v2 on v1

v2 whole, which is shorter than its diff:
```python
import jax
import jax.numpy as jnp
from jax import lax
from jax.experimental import pallas as pl
from jax.experimental.pallas import tpu as pltpu
from jax.sharding import PartitionSpec as P

MESH = pl.DeviceIdType.MESH
BF = jnp.bfloat16
F32 = jnp.float32

NX, NY, NZ = 4, 4, 8
D, FF, TOK, TOP, CAP = 2048, 768, 64, 8, 9
HALF = D // 2
BLK = 16 * CAP
ROWS = NY * BLK
SHARE = FF // NX
QC = 256
NQ = HALF // QC
WIDE = 512
ORDER = (2, 6, 4, 3, 7, 5, 1, 0)


def dot(a, b, ca, cb):
    return lax.dot_general(a, b, (((ca,), (cb,)), ((), ())), preferred_element_type=F32)


def kernel(
    tok, cot, ids, gates, wg_h, wu_h, wd_h,
    mixed_o, gtok_o, gw_o,
    T, S, meta_s, meta_r, pos, gat, yb, xin, wg, wu, wd, act, ret, zr, G, xr1, xr2, tw,
    w_sem, tws, twr, tls, ms, mr, zs, zrv, ys, yr, rs, rr, zbs, zbr, xs, xrv, os_, orv, ol,
):
    x = lax.axis_index("dp")
    e = lax.axis_index("expert")
    y, z, c = e // 16, lax.rem(e // 2, NZ), lax.rem(e, 2)

    def at(dx, dy, dz, dc):
        return (
            lax.rem(x + dx + NX, NX),
            (lax.rem(y + dy + NY, NY) * NZ + lax.rem(z + dz + NZ, NZ)) * 2 + lax.rem(c + dc, 2),
        )

    def remote(src, dst, ssem, rsem, where):
        return pltpu.make_async_remote_copy(
            src_ref=src, dst_ref=dst, send_sem=ssem, recv_sem=rsem,
            device_id=where, device_id_type=MESH,
        )

    w_in = [
        pltpu.make_async_copy(src, dst, w_sem.at[i])
        for i, (src, dst) in enumerate(((wg_h, wg), (wu_h, wu), (wd_h, wd)))
    ]
    for cp in w_in:
        cp.start()

    idv = ids[...]
    place = ((idv >> 1) & 7) * 8 + (idv >> 4) * 2 + (idv & 1)
    row = lax.broadcasted_iota(jnp.int32, (64, TOK), 0)
    named = jnp.zeros((64, TOK), F32)
    gated = jnp.zeros((64, TOK), F32)
    for k in range(TOP):
        hit = place[k : k + 1, :] == row
        named = named + jnp.where(hit, 1.0, 0.0)
        gated = gated + jnp.where(hit, gates[k : k + 1, :], 0.0)
    t0 = lax.broadcasted_iota(jnp.int32, (TOK, 128), 0)
    l0 = lax.broadcasted_iota(jnp.int32, (TOK, 128), 1) - TOK * c
    same = jnp.where(t0 == l0, 1.0, 0.0).astype(BF)
    upto = jnp.where(t0 <= l0, jnp.where(l0 < TOK, 1.0, 0.0), 0.0).astype(BF)
    named = named.astype(BF)
    rank = dot(named, upto, 1, 0) * dot(named, same, 1, 0)
    gate_t = dot(gated.astype(BF), same, 1, 0)
    for k in range(NZ):
        meta_s[k, 0:8, :] = rank[k * 8 : k * 8 + 8]
        meta_s[k, 8:16, :] = gate_t[k * 8 : k * 8 + 8]

    greet = [(0, 0, dz, dc) for dz in range(NZ) for dc in range(2) if dz or dc]
    greet += [(0, dy, 0, dc) for dy in range(1, NY) for dc in range(2)]
    greet += [(1, 0, 0, 0), (-1, 0, 0, 0)]
    bar = pltpu.get_barrier_semaphore()
    for g in greet:
        pl.semaphore_signal(bar, inc=1, device_id=at(*g), device_id_type=MESH)
    pl.semaphore_wait(bar, len(greet))

    def zrow(dz, lo=0, n=128):
        return pl.ds(pl.multiple_of(lax.rem(z + dz + NZ, NZ) * 128 + lo, 16), n)

    mine = pl.ds(pl.multiple_of(c * HALF, HALF), HALF)
    other = pl.ds(pl.multiple_of((1 - c) * HALF, HALF), HALF)

    swaps, keeps = [], []
    for a, src in enumerate((tok, cot)):
        rows = pl.ds(pl.multiple_of(z * 128 + c * TOK, TOK), TOK)
        cp = remote(src.at[:, other], T.at[a, rows, :], tws.at[a], twr.at[a], at(0, 0, 0, 1))
        cp.start()
        swaps.append(cp)
        cp = pltpu.make_async_copy(src.at[:, mine], T.at[a, rows, :], tls.at[a])
        cp.start()
        keeps.append(cp)

    metas = []
    for dz in (1, 7, 2, 6, 3, 5, 4, 0):
        for dc in (0, 1):
            src = meta_s.at[lax.rem(z + dz, NZ)]
            dst = meta_r.at[z * 2 + c]
            if dz == 0 and dc == 0:
                cp = pltpu.make_async_copy(src, dst, mr.at[0, 0])
            else:
                cp = remote(src, dst, ms.at[dz, dc], mr.at[dz, dc], at(0, 0, dz, dc))
            cp.start()
            metas.append((cp, dz or dc))

    NP = 2 * NQ

    def zcopy(p, s, way):
        a = p // NQ
        cols = pl.ds((p % NQ) * QC, QC)
        rows = zrow(-s * way) if s < 3 else zrow(-3 * way, 0 if way == 1 else 64, 64)
        i = 0 if way == 1 else 1
        return remote(
            T.at[a, rows, cols], T.at[a, rows, cols],
            zs.at[p, s, i], zrv.at[p, s, i], at(0, 0, way, 0),
        )

    zc = {(p, s, w): zcopy(p, s, w) for p in range(NP) for s in range(4) for w in (1, -1)}

    def zstart(p, s):
        for w in (1, -1):
            if s:
                zc[p, s - 1, w].wait_recv()
            zc[p, s, w].start()

    def target(r):
        return at(0, r // 2, 0, r % 2)

    my_rows = pl.ds(pl.multiple_of(y * BLK, 16), BLK)

    def ycopy(p, r):
        a, q = p // NQ, p % NQ
        src = yb.at[a, pl.ds(r * BLK, BLK), pl.ds(q * QC, QC)]
        dst = xin.at[a, my_rows, pl.ds(pl.multiple_of(c * HALF + q * QC, QC), QC)]
        if r == 0:
            return pltpu.make_async_copy(src, dst, yr.at[p, 0])
        return remote(src, dst, ys.at[p, r], yr.at[p, r], target(r))

    yc = {(p, r): ycopy(p, r) for p in range(NP) for r in range(8)}

    def select(p, dy):
        a, q = p // NQ, p % NQ
        block = slice(2 * dy * BLK, 2 * (dy + 1) * BLK)
        cols = slice(q * QC, (q + 1) * QC)
        yb[a, block, cols] = dot(S[a, block, :], T[a, :, cols], 1, 0).astype(BF)
        yc[p, 2 * dy + 1].start()
        yc[p, 2 * dy].start()

    for a in range(2):
        swaps[a].wait_recv()
        keeps[a].wait()
    zstart(0, 0)
    zstart(0, 1)
    zstart(1, 0)

    for cp, far in metas:
        if far:
            cp.wait_recv()
        else:
            cp.wait()
    lane8 = lax.broadcasted_iota(jnp.int32, (8, 128), 1)
    for k in range(NZ):
        enc = meta_r[2 * k, 0:8, :] + meta_r[2 * k + 1, 0:8, :]
        base = jnp.where(lane8 < TOK, 2.0 * k * CAP - 1.0, (2.0 * k + 1.0) * CAP - 1.0)
        pos[:, k * 128 : (k + 1) * 128] = jnp.where(enc > 0.5, enc + base, -1.0)
        gat[:, k * 128 : (k + 1) * 128] = meta_r[2 * k, 8:16, :] + meta_r[2 * k + 1, 8:16, :]
    row16 = lax.broadcasted_iota(jnp.int32, (16, 16 * TOK), 0).astype(F32)

    def build(r, carry):
        j = lax.rem(y + r // 2, NY) * 2 + lax.rem(c + r, 2)
        prow = pos[pl.ds(j, 1), :]
        grow = gat[pl.ds(j, 1), :]
        for i in range(BLK // 16):
            hit = row16 + float(16 * i) == prow
            at_rows = pl.ds(pl.multiple_of(r * BLK + 16 * i, 16), 16)
            S[0, at_rows, :] = jnp.where(hit, 1.0, 0.0).astype(BF)
            S[1, at_rows, :] = jnp.where(hit, grow, 0.0).astype(BF)
        return carry

    lax.fori_loop(0, 8, build, 0)

    def arrived(p):
        for r in range(8):
            if r:
                yc[p, r].wait_recv()
                yc[p, r].wait_send()
            else:
                yc[p, r].wait()

    HR = ROWS // 2

    def forward(n):
        def part(i, carry):
            rows = pl.ds(pl.multiple_of(i * HR, 16), HR)
            cols = slice(n * 256, (n + 1) * 256)
            v = xin[0, rows, :]
            g = dot(v, wg[:, cols], 1, 0)
            u = dot(v, wu[:, cols], 1, 0)
            sg = jax.nn.sigmoid(g)
            silu = g * sg
            act[0, rows, cols] = (silu * u).astype(BF)
            act[1, rows, cols] = (u * sg * (1.0 + g * (1.0 - sg))).astype(BF)
            act[2, rows, cols] = silu.astype(BF)
            return carry

        lax.fori_loop(0, 2, part, 0)

    DY = (1, 3, 2, 0)
    for t in range(2, NP + 4):
        for i in range(4):
            k = t - 3 + i
            if 0 <= k < NP:
                zstart(k, t - k)
            if i == 0 and t >= 4:
                for w in (1, -1):
                    zc[t - 4, 3, w].wait_recv()
            if t >= 4:
                select(t - 4, DY[i])
        if t == NP:
            for p in range(NQ):
                arrived(p)
            for cp in w_in:
                cp.wait()
        if NP <= t < NP + FF // 256:
            forward(t - NP)

    def give_back(a, q, h, rows):
        for k in range(NY):
            r = lax.rem(k - y + NY, NY) * 2 + lax.rem(h - c + 2, 2)
            yb[a, pl.ds(pl.multiple_of(r * BLK, 16), BLK), q * WIDE : (q + 1) * WIDE] = (
                rows[k * BLK : (k + 1) * BLK].astype(BF)
            )

    def rcopy(a, q, r):
        cols = pl.ds(q * QC, QC)
        there = (NY - r // 2) % NY * 2 + r % 2
        src = yb.at[a, pl.ds(r * BLK, BLK), cols]
        dst = ret.at[a, pl.ds(there * BLK, BLK), cols]
        if r == 0:
            return pltpu.make_async_copy(src, dst, rr.at[a, q, 0])
        return remote(src, dst, rs.at[a, q, r], rr.at[a, q, r], target(r))

    rc = {(a, q, r): rcopy(a, q, r) for a in range(2) for q in range(NQ) for r in range(8)}

    NW = WIDE // QC
    for q in range(HALF // WIDE):
        for h in range(2):
            n = h * HALF + q * WIDE
            give_back(0, q, h, dot(act[0], wd[:, n : n + WIDE], 1, 0))
        for i in range(q * NW, (q + 1) * NW):
            for r in ORDER:
                rc[0, i, r].start()

    def xshare(dx):
        return lax.rem(x + dx + NX, NX)

    SH2 = SHARE // 2

    def piece(n):
        if n < 2:
            return n, slice(0, HALF)
        return 2, slice((n - 2) * QC, (n - 1) * QC)

    PIECES = 2 + NQ

    def xcopy1(n, way):
        i = 0 if way == 1 else 1
        m, cols = piece(n)
        return remote(
            G.at[xshare(2), m, :, pl.ds(i * SH2, SH2), cols], xr1.at[i, m, :, :, cols],
            xs.at[0, n, i], xrv.at[0, n, i], at(way, 0, 0, 0),
        )

    def xcopy2(n, way):
        i = 0 if way == 1 else 1
        m, cols = piece(n)
        return remote(
            G.at[xshare(way), m, :, :, cols], xr2.at[i, m, :, :, cols],
            xs.at[1, n, i], xrv.at[1, n, i], at(way, 0, 0, 0),
        )

    xc1 = {(n, w): xcopy1(n, w) for n in range(PIECES) for w in (1, -1)}
    xc2 = {(n, w): xcopy2(n, w) for n in range(PIECES) for w in (1, -1)}

    def product(m, b, k, h, cols, at_cols):
        for hf in range(2):
            v = dot(act[k, :, hf * 384 : (hf + 1) * 384], xin[b, :, cols], 0, 0).astype(BF)
            G[2 * hf, m, h, :, at_cols] = v[:SHARE]
            G[2 * hf + 1, m, h, :, at_cols] = v[SHARE:]

    def weights(m, b, k):
        def part(i, carry):
            here = pl.ds(pl.multiple_of(i * WIDE, WIDE), WIDE)
            for h in range(2):
                cols = pl.ds(pl.multiple_of(h * HALF + i * WIDE, WIDE), WIDE)
                product(m, b, k, h, cols, here)
            return carry

        lax.fori_loop(0, HALF // WIDE, part, 0)
        for w in (1, -1):
            xc1[m, w].start()

    def xadd(n):
        m, cols = piece(n)
        for i, w in enumerate((1, -1)):
            xc1[n, w].wait_recv()
            rows = pl.ds(i * SH2, SH2)
            d = xshare(w)
            for h in range(2):
                G[d, m, h, rows, cols] = (
                    G[d, m, h, rows, cols].astype(F32) + xr1[i, m, h, :, cols].astype(F32)
                ).astype(BF)
            xc2[n, w].start()

    def xfinish(m):
        for n in range(PIECES):
            if piece(n)[0] == m:
                for w in (1, -1):
                    xc2[n, w].wait_recv()
        own = xshare(0)
        for h in range(2):
            G[own, m, h] = (
                G[own, m, h].astype(F32) + xr2[0, m, h].astype(F32) + xr2[1, m, h].astype(F32)
            ).astype(BF)
            cp = pltpu.make_async_copy(
                G.at[own, m, h], gw_o.at[m, :, pl.ds(h * HALF, HALF)], ol.at[4 + 2 * m + h]
            )
            cp.start()
            tail.append(cp)

    tail = []
    for i in range(NQ):
        arrived(NQ + i)
        for h in range(2):
            n = h * HALF + i * QC
            product(2, 1, 0, h, slice(n, n + QC), slice(i * QC, (i + 1) * QC))
        for w in (1, -1):
            xc1[2 + i, w].start()
        if i:
            xadd(1 + i)

    def backward(i, carry):
        cols = pl.ds(pl.multiple_of(i * 256, 256), 256)
        g = dot(xin[1], wd[cols, :], 1, 1)
        act[1, :, cols] = (g * act[1, :, cols].astype(F32)).astype(BF)
        act[2, :, cols] = (g * act[2, :, cols].astype(F32)).astype(BF)
        return carry

    lax.fori_loop(0, FF // 256, backward, 0)
    weights(0, 0, 1)
    weights(1, 0, 2)
    xadd(1 + NQ)
    for q in range(HALF // WIDE):
        for h in range(2):
            n = h * HALF + q * WIDE
            give_back(
                1, q, h,
                dot(act[1], wg[n : n + WIDE, :], 1, 1) + dot(act[2], wu[n : n + WIDE, :], 1, 1),
            )
        for i in range(q * NW, (q + 1) * NW):
            for r in ORDER:
                rc[1, i, r].start()

    for a in range(2):
        swaps[a].wait_send()
    for key in zc:
        zc[key].wait_send()

    def bcopy(k, s, way):
        a, q = k // NQ, k % NQ
        i = 0 if way == 1 else 1
        cols = pl.ds(q * QC, QC)
        rows = zrow((4 - s) * way) if s else zrow(4, 64 * i, 64)
        dst = zr.at[a, i, s, :, cols] if s else zr.at[a, i, 0, pl.ds(0, 64), cols]
        return remote(
            T.at[a, rows, cols], dst, zbs.at[k, s, i], zbr.at[k, s, i], at(0, 0, way, 0)
        )

    bc = {(k, s, w): bcopy(k, s, w) for k in range(NP) for s in range(4) for w in (1, -1)}

    def combine(k):
        a, q = k // NQ, k % NQ
        for r in range(8):
            if r:
                rc[a, q, r].wait_recv()
            else:
                rc[a, q, r].wait()
        cols = slice(q * QC, (q + 1) * QC)
        for n in range(2):
            half = slice(n * 512, (n + 1) * 512)
            T[a, half, cols] = dot(S[1 - a, :, half], ret[a, :, cols], 0, 0).astype(BF)
        for w in (1, -1):
            bc[k, 0, w].start()

    def pass_on(k, s):
        a, q = k // NQ, k % NQ
        cols = slice(q * QC, (q + 1) * QC)
        for i, w in enumerate((1, -1)):
            bc[k, s - 1, w].wait_recv()
            n = 64 if s == 1 else 128
            rows = zrow((4 - s) * w, 64 * i if s == 1 else 0, n)
            T[a, rows, cols] = (
                T[a, rows, cols].astype(F32) + zr[a, i, s - 1, 0:n, cols].astype(F32)
            ).astype(BF)
            bc[k, s, w].start()

    def finish(k):
        a, q = k // NQ, k % NQ
        cols = slice(q * QC, (q + 1) * QC)
        for w in (1, -1):
            bc[k, 3, w].wait_recv()
        rows = zrow(0)
        T[a, rows, cols] = (
            T[a, rows, cols].astype(F32)
            + zr[a, 0, 3, :, cols].astype(F32)
            + zr[a, 1, 3, :, cols].astype(F32)
        ).astype(BF)

    outs = (mixed_o, gtok_o)

    def hand_over(a):
        theirs = pl.ds(pl.multiple_of(z * 128 + (1 - c) * TOK, TOK), TOK)
        ours = pl.ds(pl.multiple_of(z * 128 + c * TOK, TOK), TOK)
        cp = remote(T.at[a, theirs, :], tw.at[a], os_.at[a], orv.at[a], at(0, 0, 0, 1))
        cp.start()
        keep = pltpu.make_async_copy(T.at[a, ours, :], outs[a].at[:, mine], ol.at[a])
        keep.start()
        return cp, keep

    def take_over(a, pair):
        cp, keep = pair
        cp.wait_recv()
        last = pltpu.make_async_copy(tw.at[a], outs[a].at[:, other], ol.at[2 + a])
        last.start()
        tail.extend((keep, last))

    pairs = {}
    for t in range(NP + 4):
        for k in range(max(0, t - 4), min(t, NP)):
            if t - k < 4:
                pass_on(k, t - k)
            else:
                finish(k)
                if k % NQ == NQ - 1:
                    pairs[k // NQ] = hand_over(k // NQ)
        if t < NP:
            combine(t)
        if t in (1, 2):
            xadd(t - 1)
        if t == NP - 2:
            xfinish(2)
        if t == NP:
            take_over(0, pairs[0])
            xfinish(0)
    take_over(1, pairs[1])
    xfinish(1)

    for cp, far in metas:
        if far:
            cp.wait_send()
    for a in range(2):
        for q in range(NQ):
            for r in range(1, 8):
                rc[a, q, r].wait_send()
    for key in bc:
        bc[key].wait_send()
    for a in range(2):
        pairs[a][0].wait_send()
    for key in xc1:
        xc1[key].wait_send()
        xc2[key].wait_send()
    for cp in tail:
        cp.wait()


def place_outputs(a, b, g, a_o, b_o, g_o, va, vb, vg, s_in, s_out):
    moves = [(g.at[m], vg.at[m], g_o.at[m]) for m in range(3)] + [(a, va, a_o), (b, vb, b_o)]
    into = [pltpu.make_async_copy(u, v, s_in.at[i]) for i, (u, v, _) in enumerate(moves)]
    out = [pltpu.make_async_copy(v, w, s_out.at[i]) for i, (_, v, w) in enumerate(moves)]
    for cp in into:
        cp.start()
    for cp, nxt in zip(into, out):
        cp.wait()
        nxt.start()
    for cp in out:
        cp.wait()


def local(tokens, expert_ids, gates, cotangent, w_gate, w_up, w_down):
    vmem = pl.BlockSpec(memory_space=pltpu.VMEM)
    hbm = pl.BlockSpec(memory_space=pl.ANY)
    dma = pltpu.SemaphoreType.DMA
    shapes = (
        jax.ShapeDtypeStruct((TOK, D), BF),
        jax.ShapeDtypeStruct((TOK, D), BF),
        jax.ShapeDtypeStruct((3, SHARE, D), BF),
    )
    results = pl.pallas_call(
        kernel,
        out_shape=shapes,
        in_specs=[vmem] * 4 + [hbm] * 3,
        out_specs=(hbm, hbm, hbm),
        scratch_shapes=[
            pltpu.VMEM((2, 16 * TOK, HALF), BF),
            pltpu.VMEM((2, 8 * BLK, 16 * TOK), BF),
            pltpu.VMEM((NZ, 16, 128), F32),
            pltpu.VMEM((2 * NZ, 16, 128), F32),
            pltpu.VMEM((8, 16 * TOK), F32),
            pltpu.VMEM((8, 16 * TOK), F32),
            pltpu.VMEM((2, 8 * BLK, HALF), BF),
            pltpu.VMEM((2, ROWS, D), BF),
            pltpu.VMEM((D, FF), BF),
            pltpu.VMEM((D, FF), BF),
            pltpu.VMEM((FF, D), BF),
            pltpu.VMEM((3, ROWS, FF), BF),
            pltpu.VMEM((2, 8 * BLK, HALF), BF),
            pltpu.VMEM((2, 2, 4, 128, HALF), BF),
            pltpu.VMEM((NX, 3, 2, SHARE, HALF), BF),
            pltpu.VMEM((2, 3, 2, SHARE // 2, HALF), BF),
            pltpu.VMEM((2, 3, 2, SHARE, HALF), BF),
            pltpu.VMEM((2, TOK, HALF), BF),
            dma((3,)), dma((2,)), dma((2,)), dma((2,)),
            dma((NZ, 2)), dma((NZ, 2)),
            dma((2 * NQ, 4, 2)), dma((2 * NQ, 4, 2)),
            dma((2 * NQ, 8)), dma((2 * NQ, 8)),
            dma((2, NQ, 8)), dma((2, NQ, 8)),
            dma((2 * NQ, 4, 2)), dma((2 * NQ, 4, 2)),
            dma((2, 2 + NQ, 2)), dma((2, 2 + NQ, 2)),
            dma((2,)), dma((2,)), dma((10,)),
        ],
        compiler_params=pltpu.CompilerParams(
            collective_id=0, has_side_effects=True, vmem_limit_bytes=60 * 2**20
        ),
        cost_estimate=pl.CostEstimate(
            flops=30_000_000_000, bytes_accessed=20_000_000, transcendentals=450_000
        ),
        name="moe",
    )(tokens, cotangent, expert_ids.T, gates.T, w_gate[0], w_up[0], w_down[0])
    mixed, grad_tokens, grads = pl.pallas_call(
        place_outputs,
        out_shape=shapes,
        in_specs=[hbm] * 3,
        out_specs=(hbm, hbm, hbm),
        scratch_shapes=[
            pltpu.VMEM((TOK, D), BF),
            pltpu.VMEM((TOK, D), BF),
            pltpu.VMEM((3, SHARE, D), BF),
            dma((5,)), dma((5,)),
        ],
        name="place_outputs",
    )(*results)
    return mixed, grad_tokens, grads.transpose(1, 0, 2)[None]


def solution(mesh):
    return jax.shard_map(
        local,
        mesh=mesh,
        in_specs=(
            P(("dp", "expert"), None),
            P(("dp", "expert"), None),
            P(("dp", "expert"), None),
            P(("dp", "expert"), None),
            P("expert", None, None),
            P("expert", None, None),
            P("expert", None, None),
        ),
        out_specs=(
            P(("dp", "expert"), None),
            P(("dp", "expert"), None),
            P("expert", "dp", None, None),
        ),
        check_vma=False,
    )
```

time: 186 us -> 169 us (0.909)
  local copies, waits for them, and re-layouts: 9.46 us -> 0 us
  Pallas kernels: 176 us -> 168 us
    unnamed x5 -> x0, local copies, waits for them, and re-layouts: 9.46 us -> none
    pallas_call x1 -> x2, Pallas kernels: 176 us -> 168 us  [the longest x1 165 us: local(): pl.pallas_call(kernel, out_shape=shapes, in_specs=[vmem] * 4 + [hbm] * 3,...]
where the time goes in v2:
time: 169 us
  Pallas kernels  168 us (99%)
    pallas_call x1, Pallas kernels, local(): pl.pallas_call(kernel, out_shape=shapes, in_specs=[vmem] * 4 + [hbm] * 3,...  165 us

profile of v2, /device:TPU:1, one launch (start us, length us, event | category | flops | bytes accessed | tf_op | source)
XLA Modules:
  0.0 169.0 jit_solution(12313378218693497513)
XLA Ops:
  0.6 165.4 %moe.1 = (bf16[64,2048]{1,0:T(8,128)(2,1)}, bf16[64,2048]{1,0:T(8,128)(2,1)}, bf16[3,192,2048]{2,1,0:T(8,128)(2,1)}) custom-call(bf16[64,2048]{1,0:T(8,128)(2,1)} %tok.1, bf16[64,2048]{1,0:T(8,128)(2,1)} %cot.1, s32[8,64]{1,0:T(8,128)} %bitcast.12, f32[8,64]{1,0:T(8,128)} %bitcast.13, bf16[2048,768]{1,0:T(8,128)(2,1)} %bitcast.8, bf16[2048,768]{1,0:T(8,128)(2,1)} %bitcast.9, ...), custom_call_target="tpu_custom_call" | custom-call | flops 30000001024 | bytes 20000000 | tf_op jit(solution)/shard_map/moe/pallas_call | solution.py:505
  166.0 2.8 %place_outputs.1 = (bf16[64,2048]{1,0:T(8,128)(2,1)}, bf16[64,2048]{1,0:T(8,128)(2,1)}, bf16[3,192,2048]{2,1,0:T(8,128)(2,1)}) custom-call(bf16[64,2048]{1,0:T(8,128)(2,1)} %get-tuple-element.9.a, bf16[64,2048]{1,0:T(8,128)(2,1)} %get-tuple-element.10.b, bf16[3,192,2048]{2,1,0:T(8,128)(2,1)} %get-tuple-element.11.g), custom_call_target="tpu_custom_call" | custom-call | tf_op jit(solution)/shard_map/place_outputs/pallas_call | solution.py:546

commit v3 on v2

--- a/solution.py
+++ b/solution.py
@@ -17,19 +17,41 @@
 SHARE = FF // NX
 QC = 256
 NQ = HALF // QC
+FULL = [(n * QC, QC) for n in range(NQ)]
+OUT = [(0, a, b) for a, b in [(0, 128), (128, 128)] + FULL[1:]] + [(1, a, b) for a, b in FULL]
+BACK = [(0, a, b) for a, b in FULL] + [(1, a, b) for a, b in FULL[:-1] + [(768, 128), (896, 128)]]
+NT = len(OUT) - NQ
 WIDE = 512
 ORDER = (2, 6, 4, 3, 7, 5, 1, 0)
 
 
 def dot(a, b, ca, cb):
     return lax.dot_general(a, b, (((ca,), (cb,)), ((), ())), preferred_element_type=F32)
+
+
+class Both:
+    def __init__(self, *copies):
+        self.copies = copies
+
+    def start(self):
+        for cp in self.copies:
+            cp.start()
+
+    def wait_recv(self):
+        for cp in self.copies:
+            cp.wait_recv()
+
+    def wait_send(self):
+        for cp in self.copies:
+            cp.wait_send()
 
 
 def kernel(
     tok, cot, ids, gates, wg_h, wu_h, wd_h,
     mixed_o, gtok_o, gw_o,
-    T, S, meta_s, meta_r, pos, gat, yb, xin, wg, wu, wd, act, ret, zr, G, xr1, xr2, tw,
-    w_sem, tws, twr, tls, ms, mr, zs, zrv, ys, yr, rs, rr, zbs, zbr, xs, xrv, os_, orv, ol,
+    T, S, meta_s, meta_r, pos, gat, yb, xin, wg, wu, wd, act, ret, zr, zl, G, xr1, xr2, tw, ob,
+    w_sem, fs, fr, tws, twr, tls, ms, mr, zs, zrv, ys, yr, rs, rr, zbs, zbr, zls, zlr, xs, xrv,
+    os_, orv, ol,
 ):
     x = lax.axis_index("dp")
     e = lax.axis_index("expert")
@@ -88,13 +110,28 @@
     mine = pl.ds(pl.multiple_of(c * HALF, HALF), HALF)
     other = pl.ds(pl.multiple_of((1 - c) * HALF, HALF), HALF)
 
+    my_slot = pl.ds(pl.multiple_of(z * 128 + c * TOK, TOK), TOK)
+
+    def first(way):
+        i = 0 if way == 1 else 1
+        _, lo, n = OUT[0]
+        return Both(*(
+            remote(
+                tok.at[:, pl.ds(pl.multiple_of(lax.rem(c + dc, 2) * HALF + lo, 128), n)],
+                T.at[0, my_slot, pl.ds(lo, n)], fs.at[i, dc], fr.at[i, dc], at(0, 0, way, dc),
+            )
+            for dc in range(2)
+        ))
+
+    begin = {w: first(w) for w in (1, -1)}
+    for w in (1, -1):
+        begin[w].start()
     swaps, keeps = [], []
     for a, src in enumerate((tok, cot)):
-        rows = pl.ds(pl.multiple_of(z * 128 + c * TOK, TOK), TOK)
-        cp = remote(src.at[:, other], T.at[a, rows, :], tws.at[a], twr.at[a], at(0, 0, 0, 1))
+        cp = remote(src.at[:, other], T.at[a, my_slot, :], tws.at[a], twr.at[a], at(0, 0, 0, 1))
         cp.start()
         swaps.append(cp)
-        cp = pltpu.make_async_copy(src.at[:, mine], T.at[a, rows, :], tls.at[a])
+        cp = pltpu.make_async_copy(src.at[:, mine], T.at[a, my_slot, :], tls.at[a])
         cp.start()
         keeps.append(cp)
 
@@ -110,11 +147,13 @@
             cp.start()
             metas.append((cp, dz or dc))
 
-    NP = 2 * NQ
+    NP = len(OUT)
 
     def zcopy(p, s, way):
-        a = p // NQ
-        cols = pl.ds((p % NQ) * QC, QC)
+        if p == 0 and s == 0:
+            return begin[way]
+        a, lo, n = OUT[p]
+        cols = pl.ds(lo, n)
         rows = zrow(-s * way) if s < 3 else zrow(-3 * way, 0 if way == 1 else 64, 64)
         i = 0 if way == 1 else 1
         return remote(
@@ -136,9 +175,9 @@
     my_rows = pl.ds(pl.multiple_of(y * BLK, 16), BLK)
 
     def ycopy(p, r):
-        a, q = p // NQ, p % NQ
-        src = yb.at[a, pl.ds(r * BLK, BLK), pl.ds(q * QC, QC)]
-        dst = xin.at[a, my_rows, pl.ds(pl.multiple_of(c * HALF + q * QC, QC), QC)]
+        a, lo, n = OUT[p]
+        src = yb.at[a, pl.ds(r * BLK, BLK), pl.ds(lo, n)]
+        dst = xin.at[a, my_rows, pl.ds(pl.multiple_of(c * HALF + lo, 128), n)]
         if r == 0:
             return pltpu.make_async_copy(src, dst, yr.at[p, 0])
         return remote(src, dst, ys.at[p, r], yr.at[p, r], target(r))
@@ -146,9 +185,9 @@
     yc = {(p, r): ycopy(p, r) for p in range(NP) for r in range(8)}
 
     def select(p, dy):
-        a, q = p // NQ, p % NQ
+        a, lo, n = OUT[p]
         block = slice(2 * dy * BLK, 2 * (dy + 1) * BLK)
-        cols = slice(q * QC, (q + 1) * QC)
+        cols = slice(lo, lo + n)
         yb[a, block, cols] = dot(S[a, block, :], T[a, :, cols], 1, 0).astype(BF)
         yc[p, 2 * dy + 1].start()
         yc[p, 2 * dy].start()
@@ -156,24 +195,24 @@
     for a in range(2):
         swaps[a].wait_recv()
         keeps[a].wait()
-    zstart(0, 0)
+    zstart(1, 0)
     zstart(0, 1)
-    zstart(1, 0)
-
-    for cp, far in metas:
-        if far:
-            cp.wait_recv()
-        else:
-            cp.wait()
-    lane8 = lax.broadcasted_iota(jnp.int32, (8, 128), 1)
-    for k in range(NZ):
-        enc = meta_r[2 * k, 0:8, :] + meta_r[2 * k + 1, 0:8, :]
-        base = jnp.where(lane8 < TOK, 2.0 * k * CAP - 1.0, (2.0 * k + 1.0) * CAP - 1.0)
-        pos[:, k * 128 : (k + 1) * 128] = jnp.where(enc > 0.5, enc + base, -1.0)
-        gat[:, k * 128 : (k + 1) * 128] = meta_r[2 * k, 8:16, :] + meta_r[2 * k + 1, 8:16, :]
-    row16 = lax.broadcasted_iota(jnp.int32, (16, 16 * TOK), 0).astype(F32)
+
+    def places():
+        for cp, far in metas:
+            if far:
+                cp.wait_recv()
+            else:
+                cp.wait()
+        lane8 = lax.broadcasted_iota(jnp.int32, (8, 128), 1)
+        for k in range(NZ):
+            enc = meta_r[2 * k, 0:8, :] + meta_r[2 * k + 1, 0:8, :]
+            base = jnp.where(lane8 < TOK, 2.0 * k * CAP - 1.0, (2.0 * k + 1.0) * CAP - 1.0)
+            pos[:, k * 128 : (k + 1) * 128] = jnp.where(enc > 0.5, enc + base, -1.0)
+            gat[:, k * 128 : (k + 1) * 128] = meta_r[2 * k, 8:16, :] + meta_r[2 * k + 1, 8:16, :]
 
     def build(r, carry):
+        row16 = lax.broadcasted_iota(jnp.int32, (16, 16 * TOK), 0).astype(F32)
         j = lax.rem(y + r // 2, NY) * 2 + lax.rem(c + r, 2)
         prow = pos[pl.ds(j, 1), :]
         grow = gat[pl.ds(j, 1), :]
@@ -183,8 +222,6 @@
             S[0, at_rows, :] = jnp.where(hit, 1.0, 0.0).astype(BF)
             S[1, at_rows, :] = jnp.where(hit, grow, 0.0).astype(BF)
         return carry
-
-    lax.fori_loop(0, 8, build, 0)
 
     def arrived(p):
         for r in range(8):
@@ -214,22 +251,26 @@
 
     DY = (1, 3, 2, 0)
     for t in range(2, NP + 4):
+        if t >= 4:
+            for w in (1, -1):
+                zc[t - 4, 3, w].wait_recv()
         for i in range(4):
             k = t - 3 + i
+            if t >= 4:
+                select(t - 4, DY[i])
             if 0 <= k < NP:
                 zstart(k, t - k)
-            if i == 0 and t >= 4:
-                for w in (1, -1):
-                    zc[t - 4, 3, w].wait_recv()
-            if t >= 4:
-                select(t - 4, DY[i])
-        if t == NP:
-            for p in range(NQ):
+        if t == 2:
+            places()
+        if t == 3:
+            lax.fori_loop(0, 8, build, 0)
+        if t == NT + 4:
+            for p in range(NT):
                 arrived(p)
             for cp in w_in:
                 cp.wait()
-        if NP <= t < NP + FF // 256:
-            forward(t - NP)
+        if NT + 4 <= t < NT + 4 + FF // 256:
+            forward(t - NT - 4)
 
     def give_back(a, q, h, rows):
         for k in range(NY):
@@ -238,25 +279,30 @@
                 rows[k * BLK : (k + 1) * BLK].astype(BF)
             )
 
-    def rcopy(a, q, r):
-        cols = pl.ds(q * QC, QC)
+    def rcopy(k, r):
+        a, lo, n = BACK[k]
+        cols = pl.ds(lo, n)
         there = (NY - r // 2) % NY * 2 + r % 2
         src = yb.at[a, pl.ds(r * BLK, BLK), cols]
         dst = ret.at[a, pl.ds(there * BLK, BLK), cols]
         if r == 0:
-            return pltpu.make_async_copy(src, dst, rr.at[a, q, 0])
-        return remote(src, dst, rs.at[a, q, r], rr.at[a, q, r], target(r))
-
-    rc = {(a, q, r): rcopy(a, q, r) for a in range(2) for q in range(NQ) for r in range(8)}
-
-    NW = WIDE // QC
+            return pltpu.make_async_copy(src, dst, rr.at[k, 0])
+        return remote(src, dst, rs.at[k, r], rr.at[k, r], target(r))
+
+    NB = len(BACK)
+    rc = {(k, r): rcopy(k, r) for k in range(NB) for r in range(8)}
+
+    def send_back(a, q):
+        for k in range(NB):
+            if BACK[k][0] == a and BACK[k][1] // WIDE == q:
+                for r in ORDER:
+                    rc[k, r].start()
+
     for q in range(HALF // WIDE):
         for h in range(2):
             n = h * HALF + q * WIDE
             give_back(0, q, h, dot(act[0], wd[:, n : n + WIDE], 1, 0))
-        for i in range(q * NW, (q + 1) * NW):
-            for r in ORDER:
-                rc[0, i, r].start()
+        send_back(0, q)
 
     def xshare(dx):
         return lax.rem(x + dx + NX, NX)
@@ -337,7 +383,7 @@
 
     tail = []
     for i in range(NQ):
-        arrived(NQ + i)
+        arrived(NT + i)
         for h in range(2):
             n = h * HALF + i * QC
             product(2, 1, 0, h, slice(n, n + QC), slice(i * QC, (i + 1) * QC))
@@ -364,115 +410,123 @@
                 1, q, h,
                 dot(act[1], wg[n : n + WIDE, :], 1, 1) + dot(act[2], wu[n : n + WIDE, :], 1, 1),
             )
-        for i in range(q * NW, (q + 1) * NW):
-            for r in ORDER:
-                rc[1, i, r].start()
+        send_back(1, q)
 
     for a in range(2):
         swaps[a].wait_send()
     for key in zc:
         zc[key].wait_send()
 
+    own_rows = {0: my_slot, 1: pl.ds(pl.multiple_of(z * 128 + (1 - c) * TOK, TOK), TOK)}
+
     def bcopy(k, s, way):
-        a, q = k // NQ, k % NQ
+        a, lo, n = BACK[k]
         i = 0 if way == 1 else 1
-        cols = pl.ds(q * QC, QC)
+        cols = pl.ds(lo, n)
+        if s == 3:
+            return Both(*(
+                remote(
+                    T.at[a, zrow(way, lax.rem(c + dc, 2) * TOK, TOK), cols],
+                    zl.at[a, i, c, :, cols], zls.at[k, i, dc], zlr.at[k, i, dc],
+                    at(0, 0, way, dc),
+                )
+                for dc in range(2)
+            ))
         rows = zrow((4 - s) * way) if s else zrow(4, 64 * i, 64)
         dst = zr.at[a, i, s, :, cols] if s else zr.at[a, i, 0, pl.ds(0, 64), cols]
         return remote(
             T.at[a, rows, cols], dst, zbs.at[k, s, i], zbr.at[k, s, i], at(0, 0, way, 0)
         )
 
-    bc = {(k, s, w): bcopy(k, s, w) for k in range(NP) for s in range(4) for w in (1, -1)}
+    def tcopy(k):
+        a, lo, n = BACK[k]
+        cols = pl.ds(lo, n)
+        return remote(
+            T.at[a, own_rows[1], cols], tw.at[a, :, cols], os_.at[k], orv.at[k], at(0, 0, 0, 1)
+        )
+
+    bc = {(k, s, w): bcopy(k, s, w) for k in range(NB) for s in range(4) for w in (1, -1)}
+    tc = {(k,): tcopy(k) for k in range(NB)}
 
     def combine(k):
-        a, q = k // NQ, k % NQ
+        a, lo, n = BACK[k]
         for r in range(8):
             if r:
-                rc[a, q, r].wait_recv()
+                rc[k, r].wait_recv()
             else:
-                rc[a, q, r].wait()
-        cols = slice(q * QC, (q + 1) * QC)
-        for n in range(2):
-            half = slice(n * 512, (n + 1) * 512)
+                rc[k, r].wait()
+        cols = slice(lo, lo + n)
+        for j in range(2):
+            half = slice(j * 512, (j + 1) * 512)
             T[a, half, cols] = dot(S[1 - a, :, half], ret[a, :, cols], 0, 0).astype(BF)
         for w in (1, -1):
             bc[k, 0, w].start()
+        tc[k,].start()
 
     def pass_on(k, s):
-        a, q = k // NQ, k % NQ
-        cols = slice(q * QC, (q + 1) * QC)
+        a, lo, n = BACK[k]
+        cols = slice(lo, lo + n)
         for i, w in enumerate((1, -1)):
             bc[k, s - 1, w].wait_recv()
-            n = 64 if s == 1 else 128
-            rows = zrow((4 - s) * w, 64 * i if s == 1 else 0, n)
+            m = 64 if s == 1 else 128
+            rows = zrow((4 - s) * w, 64 * i if s == 1 else 0, m)
             T[a, rows, cols] = (
-                T[a, rows, cols].astype(F32) + zr[a, i, s - 1, 0:n, cols].astype(F32)
+                T[a, rows, cols].astype(F32) + zr[a, i, s - 1, 0:m, cols].astype(F32)
             ).astype(BF)
             bc[k, s, w].start()
 
     def finish(k):
-        a, q = k // NQ, k % NQ
-        cols = slice(q * QC, (q + 1) * QC)
+        a, lo, n = BACK[k]
+        cols = slice(lo, lo + n)
         for w in (1, -1):
             bc[k, 3, w].wait_recv()
-        rows = zrow(0)
-        T[a, rows, cols] = (
-            T[a, rows, cols].astype(F32)
-            + zr[a, 0, 3, :, cols].astype(F32)
-            + zr[a, 1, 3, :, cols].astype(F32)
-        ).astype(BF)
+        tc[k,].wait_recv()
+        for h, mid in ((c, T[a, own_rows[0], cols]), (1 - c, tw[a, :, cols])):
+            ob[a, h, :, cols] = (
+                mid.astype(F32)
+                + zl[a, 0, h, :, cols].astype(F32)
+                + zl[a, 1, h, :, cols].astype(F32)
+            ).astype(BF)
 
     outs = (mixed_o, gtok_o)
 
-    def hand_over(a):
-        theirs = pl.ds(pl.multiple_of(z * 128 + (1 - c) * TOK, TOK), TOK)
-        ours = pl.ds(pl.multiple_of(z * 128 + c * TOK, TOK), TOK)
-        cp = remote(T.at[a, theirs, :], tw.at[a], os_.at[a], orv.at[a], at(0, 0, 0, 1))
-        cp.start()
-        keep = pltpu.make_async_copy(T.at[a, ours, :], outs[a].at[:, mine], ol.at[a])
-        keep.start()
-        return cp, keep
-
-    def take_over(a, pair):
-        cp, keep = pair
-        cp.wait_recv()
-        last = pltpu.make_async_copy(tw.at[a], outs[a].at[:, other], ol.at[2 + a])
-        last.start()
-        tail.extend((keep, last))
-
-    pairs = {}
-    for t in range(NP + 4):
-        for k in range(max(0, t - 4), min(t, NP)):
+    def deliver(a):
+        for h in range(2):
+            cp = pltpu.make_async_copy(
+                ob.at[a, h], outs[a].at[:, pl.ds(h * HALF, HALF)], ol.at[2 * a + h]
+            )
+            cp.start()
+            tail.append(cp)
+
+    for t in range(NB + 4):
+        for k in range(max(0, t - 4), min(t, NB)):
             if t - k < 4:
                 pass_on(k, t - k)
             else:
                 finish(k)
-                if k % NQ == NQ - 1:
-                    pairs[k // NQ] = hand_over(k // NQ)
-        if t < NP:
+                if k == NQ - 1:
+                    deliver(0)
+        if t < NB:
             combine(t)
         if t in (1, 2):
             xadd(t - 1)
-        if t == NP - 2:
+        if t == NB - 2:
             xfinish(2)
-        if t == NP:
-            take_over(0, pairs[0])
+        if t == NB:
             xfinish(0)
-    take_over(1, pairs[1])
+    deliver(1)
     xfinish(1)
 
     for cp, far in metas:
         if far:
             cp.wait_send()
-    for a in range(2):
-        for q in range(NQ):
-            for r in range(1, 8):
-                rc[a, q, r].wait_send()
+    for key in rc:
+        if key[1]:
+            rc[key].wait_send()
+    for key in tc:
+        tc[key].wait_send()
     for key in bc:
         bc[key].wait_send()
-    for a in range(2):
-        pairs[a][0].wait_send()
     for key in xc1:
         xc1[key].wait_send()
         xc2[key].wait_send()
@@ -521,19 +575,22 @@
             pltpu.VMEM((FF, D), BF),
             pltpu.VMEM((3, ROWS, FF), BF),
             pltpu.VMEM((2, 8 * BLK, HALF), BF),
-            pltpu.VMEM((2, 2, 4, 128, HALF), BF),
+            pltpu.VMEM((2, 2, 3, 128, HALF), BF),
+            pltpu.VMEM((2, 2, 2, TOK, HALF), BF),
             pltpu.VMEM((NX, 3, 2, SHARE, HALF), BF),
             pltpu.VMEM((2, 3, 2, SHARE // 2, HALF), BF),
             pltpu.VMEM((2, 3, 2, SHARE, HALF), BF),
             pltpu.VMEM((2, TOK, HALF), BF),
-            dma((3,)), dma((2,)), dma((2,)), dma((2,)),
+            pltpu.VMEM((2, 2, TOK, HALF), BF),
+            dma((3,)), dma((2, 2)), dma((2, 2)), dma((2,)), dma((2,)), dma((2,)),
             dma((NZ, 2)), dma((NZ, 2)),
-            dma((2 * NQ, 4, 2)), dma((2 * NQ, 4, 2)),
-            dma((2 * NQ, 8)), dma((2 * NQ, 8)),
-            dma((2, NQ, 8)), dma((2, NQ, 8)),
-            dma((2 * NQ, 4, 2)), dma((2 * NQ, 4, 2)),
+            dma((len(OUT), 4, 2)), dma((len(OUT), 4, 2)),
+            dma((len(OUT), 8)), dma((len(OUT), 8)),
+            dma((len(BACK), 8)), dma((len(BACK), 8)),
+            dma((len(BACK), 3, 2)), dma((len(BACK), 3, 2)),
+            dma((len(BACK), 2, 2)), dma((len(BACK), 2, 2)),
             dma((2, 2 + NQ, 2)), dma((2, 2 + NQ, 2)),
-            dma((2,)), dma((2,)), dma((10,)),
+            dma((len(BACK),)), dma((len(BACK),)), dma((10,)),
         ],
         compiler_params=pltpu.CompilerParams(
             collective_id=0, has_side_effects=True, vmem_limit_bytes=60 * 2**20

time: 169 us -> 169 us (level)
  no operation moved by 1% of the time
where the time goes in v3:
time: 169 us
  Pallas kernels  168 us (99%)
    pallas_call x1, Pallas kernels, local(): pl.pallas_call(kernel, out_shape=shapes, in_specs=[vmem] * 4 + [hbm] * 3,...  165 us

profile of v3, /device:TPU:1, one launch (start us, length us, event | category | flops | bytes accessed | tf_op | source)
XLA Modules:
  0.0 169.0 jit_solution(12344158768941745131)
XLA Ops:
  0.6 165.4 %moe.1 = (bf16[64,2048]{1,0:T(8,128)(2,1)}, bf16[64,2048]{1,0:T(8,128)(2,1)}, bf16[3,192,2048]{2,1,0:T(8,128)(2,1)}) custom-call(bf16[64,2048]{1,0:T(8,128)(2,1)} %tok.1, bf16[64,2048]{1,0:T(8,128)(2,1)} %cot.1, s32[8,64]{1,0:T(8,128)} %bitcast.12, f32[8,64]{1,0:T(8,128)} %bitcast.13, bf16[2048,768]{1,0:T(8,128)(2,1)} %bitcast.8, bf16[2048,768]{1,0:T(8,128)(2,1)} %bitcast.9, ...), custom_call_target="tpu_custom_call" | custom-call | flops 30000001024 | bytes 20000000 | tf_op jit(solution)/shard_map/moe/pallas_call | solution.py:559
  166.0 2.8 %place_outputs.1 = (bf16[64,2048]{1,0:T(8,128)(2,1)}, bf16[64,2048]{1,0:T(8,128)(2,1)}, bf16[3,192,2048]{2,1,0:T(8,128)(2,1)}) custom-call(bf16[64,2048]{1,0:T(8,128)(2,1)} %get-tuple-element.9.a, bf16[64,2048]{1,0:T(8,128)(2,1)} %get-tuple-element.10.b, bf16[3,192,2048]{2,1,0:T(8,128)(2,1)} %get-tuple-element.11.g), custom_call_target="tpu_custom_call" | custom-call | tf_op jit(solution)/shard_map/place_outputs/pallas_call | solution.py:603

commit v4 on v3

--- a/solution.py
+++ b/solution.py
@@ -264,13 +264,13 @@
             places()
         if t == 3:
             lax.fori_loop(0, 8, build, 0)
-        if t == NT + 4:
-            for p in range(NT):
-                arrived(p)
-            for cp in w_in:
-                cp.wait()
-        if NT + 4 <= t < NT + 4 + FF // 256:
-            forward(t - NT - 4)
+
+    for p in range(NT):
+        arrived(p)
+    for cp in w_in:
+        cp.wait()
+    for n in range(FF // 256):
+        forward(n)
 
     def give_back(a, q, h, rows):
         for k in range(NY):
@@ -298,7 +298,7 @@
                 for r in ORDER:
                     rc[k, r].start()
 
-    for q in range(HALF // WIDE):
+    def results(q):
         for h in range(2):
             n = h * HALF + q * WIDE
             give_back(0, q, h, dot(act[0], wd[:, n : n + WIDE], 1, 0))
@@ -391,6 +391,8 @@
             xc1[2 + i, w].start()
         if i:
             xadd(1 + i)
+        if i < HALF // WIDE:
+            results(i)
 
     def backward(i, carry):
         cols = pl.ds(pl.multiple_of(i * 256, 256), 256)
@@ -398,19 +400,6 @@
         act[1, :, cols] = (g * act[1, :, cols].astype(F32)).astype(BF)
         act[2, :, cols] = (g * act[2, :, cols].astype(F32)).astype(BF)
         return carry
-
-    lax.fori_loop(0, FF // 256, backward, 0)
-    weights(0, 0, 1)
-    weights(1, 0, 2)
-    xadd(1 + NQ)
-    for q in range(HALF // WIDE):
-        for h in range(2):
-            n = h * HALF + q * WIDE
-            give_back(
-                1, q, h,
-                dot(act[1], wg[n : n + WIDE, :], 1, 1) + dot(act[2], wu[n : n + WIDE, :], 1, 1),
-            )
-        send_back(1, q)
 
     for a in range(2):
         swaps[a].wait_send()
@@ -498,6 +487,27 @@
             cp.start()
             tail.append(cp)
 
+    def slot_grads(q):
+        for h in range(2):
+            n = h * HALF + q * WIDE
+            give_back(
+                1, q, h,
+                dot(act[1], wg[n : n + WIDE, :], 1, 1) + dot(act[2], wu[n : n + WIDE, :], 1, 1),
+            )
+        send_back(1, q)
+
+    lax.fori_loop(0, FF // 256, backward, 0)
+    xadd(1 + NQ)
+    weights(0, 0, 1)
+    between = {
+        0: lambda: weights(1, 0, 2),
+        1: lambda: slot_grads(0),
+        2: lambda: slot_grads(1),
+        3: lambda: xadd(0),
+        4: lambda: xadd(1),
+        NB - 2: lambda: xfinish(2),
+        NB + 2: lambda: xfinish(0),
+    }
     for t in range(NB + 4):
         for k in range(max(0, t - 4), min(t, NB)):
             if t - k < 4:
@@ -508,12 +518,8 @@
                     deliver(0)
         if t < NB:
             combine(t)
-        if t in (1, 2):
-            xadd(t - 1)
-        if t == NB - 2:
-            xfinish(2)
-        if t == NB:
-            xfinish(0)
+        if t in between:
+            between[t]()
     deliver(1)
     xfinish(1)
 

time: 169 us -> 162 us (0.959)
  Pallas kernels: 168 us -> 161 us
    pallas_call x1, Pallas kernels: 165 us -> 159 us  [local(): pl.pallas_call(kernel, out_shape=shapes, in_specs=[vmem] * 4 + [hbm] * 3,...]
where the time goes in v4:
time: 162 us
  Pallas kernels  161 us (99%)
    pallas_call x1, Pallas kernels, local(): pl.pallas_call(kernel, out_shape=shapes, in_specs=[vmem] * 4 + [hbm] * 3,...  159 us

profile of v4, /device:TPU:1, one launch (start us, length us, event | category | flops | bytes accessed | tf_op | source)
XLA Modules:
  0.0 162.2 jit_solution(11609443288008306977)
XLA Ops:
  0.6 158.6 %moe.1 = (bf16[64,2048]{1,0:T(8,128)(2,1)}, bf16[64,2048]{1,0:T(8,128)(2,1)}, bf16[3,192,2048]{2,1,0:T(8,128)(2,1)}) custom-call(bf16[64,2048]{1,0:T(8,128)(2,1)} %tok.1, bf16[64,2048]{1,0:T(8,128)(2,1)} %cot.1, s32[8,64]{1,0:T(8,128)} %bitcast.12, f32[8,64]{1,0:T(8,128)} %bitcast.13, bf16[2048,768]{1,0:T(8,128)(2,1)} %bitcast.8, bf16[2048,768]{1,0:T(8,128)(2,1)} %bitcast.9, ...), custom_call_target="tpu_custom_call" | custom-call | flops 30000001024 | bytes 20000000 | tf_op jit(solution)/shard_map/moe/pallas_call | solution.py:565
  159.2 2.8 %place_outputs.1 = (bf16[64,2048]{1,0:T(8,128)(2,1)}, bf16[64,2048]{1,0:T(8,128)(2,1)}, bf16[3,192,2048]{2,1,0:T(8,128)(2,1)}) custom-call(bf16[64,2048]{1,0:T(8,128)(2,1)} %get-tuple-element.9.a, bf16[64,2048]{1,0:T(8,128)(2,1)} %get-tuple-element.10.b, bf16[3,192,2048]{2,1,0:T(8,128)(2,1)} %get-tuple-element.11.g), custom_call_target="tpu_custom_call" | custom-call | tf_op jit(solution)/shard_map/place_outputs/pallas_call | solution.py:609

commit v5 on v4

--- a/solution.py
+++ b/solution.py
@@ -389,10 +389,10 @@
             product(2, 1, 0, h, slice(n, n + QC), slice(i * QC, (i + 1) * QC))
         for w in (1, -1):
             xc1[2 + i, w].start()
-        if i:
-            xadd(1 + i)
         if i < HALF // WIDE:
             results(i)
+        if i > 1:
+            xadd(i)
 
     def backward(i, carry):
         cols = pl.ds(pl.multiple_of(i * 256, 256), 256)
@@ -497,12 +497,12 @@
         send_back(1, q)
 
     lax.fori_loop(0, FF // 256, backward, 0)
+    weights(0, 0, 1)
+    xadd(NQ)
     xadd(1 + NQ)
-    weights(0, 0, 1)
     between = {
-        0: lambda: weights(1, 0, 2),
-        1: lambda: slot_grads(0),
-        2: lambda: slot_grads(1),
+        0: lambda: (weights(1, 0, 2), slot_grads(0)),
+        1: lambda: slot_grads(1),
         3: lambda: xadd(0),
         4: lambda: xadd(1),
         NB - 2: lambda: xfinish(2),

time: 162 us -> 162 us (level)
  no operation moved by 1% of the time
where the time goes in v5:
time: 162 us
  Pallas kernels  162 us (100%)
    pallas_call x1, Pallas kernels, local(): pl.pallas_call(kernel, out_shape=shapes, in_specs=[vmem] * 4 + [hbm] * 3,...  159 us

profile of v5, /device:TPU:1, one launch (start us, length us, event | category | flops | bytes accessed | tf_op | source)
XLA Modules:
  0.0 162.4 jit_solution(10301131078333492980)
XLA Ops:
  0.6 158.8 %moe.1 = (bf16[64,2048]{1,0:T(8,128)(2,1)}, bf16[64,2048]{1,0:T(8,128)(2,1)}, bf16[3,192,2048]{2,1,0:T(8,128)(2,1)}) custom-call(bf16[64,2048]{1,0:T(8,128)(2,1)} %tok.1, bf16[64,2048]{1,0:T(8,128)(2,1)} %cot.1, s32[8,64]{1,0:T(8,128)} %bitcast.12, f32[8,64]{1,0:T(8,128)} %bitcast.13, bf16[2048,768]{1,0:T(8,128)(2,1)} %bitcast.8, bf16[2048,768]{1,0:T(8,128)(2,1)} %bitcast.9, ...), custom_call_target="tpu_custom_call" | custom-call | flops 30000001024 | bytes 20000000 | tf_op jit(solution)/shard_map/moe/pallas_call | solution.py:565
  159.4 2.8 %place_outputs.1 = (bf16[64,2048]{1,0:T(8,128)(2,1)}, bf16[64,2048]{1,0:T(8,128)(2,1)}, bf16[3,192,2048]{2,1,0:T(8,128)(2,1)}) custom-call(bf16[64,2048]{1,0:T(8,128)(2,1)} %get-tuple-element.9.a, bf16[64,2048]{1,0:T(8,128)(2,1)} %get-tuple-element.10.b, bf16[3,192,2048]{2,1,0:T(8,128)(2,1)} %get-tuple-element.11.g), custom_call_target="tpu_custom_call" | custom-call | tf_op jit(solution)/shard_map/place_outputs/pallas_call | solution.py:609
